TPU v7x, 128 devices: a whole 4x4x4 slice. The times are simulated.
128 devices in a mesh: wide: 32 (over y, x, z_hi), blk: 4 (over z_lo, core).
Axes of the slice: x: 4, y: 4, z: 4 (z_hi: 2, z_lo: 2; z = z_hi * 2 + z_lo), core: 2. Of those that a mesh axis runs over, the one named last changes fastest.
Arguments:
- visual_features: bfloat16 [131072, 1152], P(('wide', 'blk')), may hold values from -0.1875 to 0.1875
- sentence_features: bfloat16 [4096, 1152], P(('wide', 'blk')), may hold values from -0.1875 to 0.1875
- true_partner_ids: int32 [131072], P(('wide', 'blk')), may hold values from 0 to 4095
- inverse_warmth: float32 [], replicated, may hold values from 90 to 110
- additive_adjust: float32 [], replicated, may hold values from -12 to -9
Outputs:
- grad_images: float32 [131072, 1152], P(('wide', 'blk'))
- grad_texts: float32 [4096, 1152], P(('wide', 'blk'))
Inputs may be any that keep to these rules, and one draw needn't show every extreme that they name: Image i is paired with text true_partner_ids[i]; a text may be paired with several images or none.
All inputs are finite; a program needn't handle non-finite values.
Results may differ from a plain program's by a relative error of at most 0.007.
Values may be sent and summed in bfloat16 or wider, within the bound.
A program may use at most 64 MiB of HBM per device.

v0:
```python
import jax
import jax.numpy as jnp
from jax import lax
from jax.sharding import PartitionSpec as P


def passed_along(array, axis, by):
    peers = lax.axis_size(axis)
    return lax.ppermute(array, axis, [(i, (i + by) % peers) for i in range(peers)])


def remaining_factors(
    visual_features, tile_length, true_partner_ids, leading_offset, inverse_warmth, additive_adjust
):
    cosine_grid = lax.dot_general(
        visual_features, tile_length, (((1,), (1,)), ((), ())), preferred_element_type=jnp.float32
    )
    sigmoid_levels = inverse_warmth * cosine_grid + additive_adjust
    columns = leading_offset + lax.iota(jnp.int32, tile_length.shape[0])
    plus_minus_ones = jnp.where(true_partner_ids[:, None] == columns[None, :], 1.0, -1.0).astype(
        jnp.float32
    )
    return (
        -inverse_warmth * plus_minus_ones * jax.nn.sigmoid(-plus_minus_ones * sigmoid_levels)
    ).astype(jnp.bfloat16)


def both_grads(visual_features, tile_length, loss_grid_scaled):
    incoming_grad_part = jnp.dot(loss_grid_scaled, tile_length, preferred_element_type=jnp.float32)
    returned_grad_part = lax.dot_general(
        loss_grid_scaled,
        visual_features,
        (((0,), (0,)), ((), ())),
        preferred_element_type=jnp.float32,
    )
    return (incoming_grad_part, returned_grad_part)


def shards(visual_features, sentence_features, true_partner_ids, inverse_warmth, additive_adjust):
    width = visual_features.shape[1]
    tdev = sentence_features.shape[0]
    n_wide = lax.axis_size("wide")
    n_blk = lax.axis_size("blk")
    wpos = lax.axis_index("wide")
    caption_group = tdev * n_blk
    held_start = jnp.zeros((tdev, width), jnp.float32)

    def step(turn, carry):
        grad_img, tile_length, held = carry
        reference_offset = (wpos - turn) % n_wide
        joined_tiles = lax.all_gather(tile_length, "blk", axis=0, tiled=True)
        loss_grid_scaled = remaining_factors(
            visual_features,
            joined_tiles,
            true_partner_ids,
            reference_offset * caption_group,
            inverse_warmth,
            additive_adjust,
        )
        incoming_grad_part, returned_grad_part = both_grads(
            visual_features, joined_tiles, loss_grid_scaled
        )
        grad_img = grad_img + incoming_grad_part
        held = held + lax.psum_scatter(
            returned_grad_part.astype(jnp.bfloat16), "blk", scatter_dimension=0, tiled=True
        ).astype(jnp.float32)
        held = passed_along(held, "wide", 1)
        tile_length = passed_along(tile_length, "wide", 1)
        return (grad_img, tile_length, held)

    start = (jnp.zeros(visual_features.shape, jnp.float32), sentence_features, held_start)
    grad_images, span_home, held = lax.fori_loop(0, n_wide, step, start)
    return (grad_images, held)


def solution(mesh):
    return jax.shard_map(
        shards,
        mesh=mesh,
        in_specs=(P(("wide", "blk"), None), P(("wide", "blk"), None), P(("wide", "blk")), P(), P()),
        out_specs=(P(("wide", "blk"), None), P(("wide", "blk"), None)),
        check_vma=False,
    )
```

profile of v0, /device:TPU:1, one launch (start us, length us, event | category | flops | bytes accessed | tf_op | source)
XLA Modules:
  0.0 1250.5 jit_solution(10544662852976132055)
XLA Ops:
  8.7 1234.5 %while.20 = (s32[]{:T(128)}, f32[1024,1152]{1,0:T(8,128)}, bf16[32,1152]{1,0:T(8,128)(2,1)S(1)}, f32[32,1152]{1,0:T(8,128)S(1)}, f32[]{:T(128)}, /*index=5*/s32[...) while((s32[]{:T(128)}, f32[1024,1152]{1,0:T(8,128)}, ...), condition=%wide.region_2.3_spmd.clone, body=%wide.region_0.2_spmd.clone.sunk | while | flops 910123136 | bytes 28145088 | solution.py:72
  8.8 7.8 all_gather.12
  25.2 16.2 %reduce-scatter.2.cloned.1.call-done = bf16[32,1152]{1,0:T(8,128)(2,1)} async-done(((bf16[128,1152]{1,0:T(8,128)(2,1)}), bf16[32,1152]{1,0:T(8,128)(2,1)}) %reduce-scatter.2.cloned.1.call-update) | async-done | bytes 73744 | tf_op jit(solution)/shard_map/while/body/eval_jaxpr/reduce_scatter | solution.py:64
  65.5 14.4 %reduce-scatter.2.cloned.1.call-done = bf16[32,1152]{1,0:T(8,128)(2,1)} async-done(((bf16[128,1152]{1,0:T(8,128)(2,1)}), bf16[32,1152]{1,0:T(8,128)(2,1)}) %reduce-scatter.2.cloned.1.call-update) | async-done | bytes 73744 | tf_op jit(solution)/shard_map/while/body/eval_jaxpr/reduce_scatter | solution.py:64
  91.9 6.8 all_gather.12
  103.9 14.3 %reduce-scatter.2.cloned.1.call-done = bf16[32,1152]{1,0:T(8,128)(2,1)} async-done(((bf16[128,1152]{1,0:T(8,128)(2,1)}), bf16[32,1152]{1,0:T(8,128)(2,1)}) %reduce-scatter.2.cloned.1.call-update) | async-done | bytes 73744 | tf_op jit(solution)/shard_map/while/body/eval_jaxpr/reduce_scatter | solution.py:64
  130.2 6.8 all_gather.12
  142.2 14.3 %reduce-scatter.2.cloned.1.call-done = bf16[32,1152]{1,0:T(8,128)(2,1)} async-done(((bf16[128,1152]{1,0:T(8,128)(2,1)}), bf16[32,1152]{1,0:T(8,128)(2,1)}) %reduce-scatter.2.cloned.1.call-update) | async-done | bytes 73744 | tf_op jit(solution)/shard_map/while/body/eval_jaxpr/reduce_scatter | solution.py:64
  168.6 6.8 all_gather.12
  180.6 14.3 %reduce-scatter.2.cloned.1.call-done = bf16[32,1152]{1,0:T(8,128)(2,1)} async-done(((bf16[128,1152]{1,0:T(8,128)(2,1)}), bf16[32,1152]{1,0:T(8,128)(2,1)}) %reduce-scatter.2.cloned.1.call-update) | async-done | bytes 73744 | tf_op jit(solution)/shard_map/while/body/eval_jaxpr/reduce_scatter | solution.py:64
  207.0 6.8 all_gather.12
  219.0 14.3 %reduce-scatter.2.cloned.1.call-done = bf16[32,1152]{1,0:T(8,128)(2,1)} async-done(((bf16[128,1152]{1,0:T(8,128)(2,1)}), bf16[32,1152]{1,0:T(8,128)(2,1)}) %reduce-scatter.2.cloned.1.call-update) | async-done | bytes 73744 | tf_op jit(solution)/shard_map/while/body/eval_jaxpr/reduce_scatter | solution.py:64
  245.3 6.8 all_gather.12
  257.4 14.3 %reduce-scatter.2.cloned.1.call-done = bf16[32,1152]{1,0:T(8,128)(2,1)} async-done(((bf16[128,1152]{1,0:T(8,128)(2,1)}), bf16[32,1152]{1,0:T(8,128)(2,1)}) %reduce-scatter.2.cloned.1.call-update) | async-done | bytes 73744 | tf_op jit(solution)/shard_map/while/body/eval_jaxpr/reduce_scatter | solution.py:64
  283.7 6.8 all_gather.12
  295.7 14.3 %reduce-scatter.2.cloned.1.call-done = bf16[32,1152]{1,0:T(8,128)(2,1)} async-done(((bf16[128,1152]{1,0:T(8,128)(2,1)}), bf16[32,1152]{1,0:T(8,128)(2,1)}) %reduce-scatter.2.cloned.1.call-update) | async-done | bytes 73744 | tf_op jit(solution)/shard_map/while/body/eval_jaxpr/reduce_scatter | solution.py:64
  322.1 6.8 all_gather.12
  334.1 14.3 %reduce-scatter.2.cloned.1.call-done = bf16[32,1152]{1,0:T(8,128)(2,1)} async-done(((bf16[128,1152]{1,0:T(8,128)(2,1)}), bf16[32,1152]{1,0:T(8,128)(2,1)}) %reduce-scatter.2.cloned.1.call-update) | async-done | bytes 73744 | tf_op jit(solution)/shard_map/while/body/eval_jaxpr/reduce_scatter | solution.py:64
  360.5 6.8 all_gather.12
  372.5 14.3 %reduce-scatter.2.cloned.1.call-done = bf16[32,1152]{1,0:T(8,128)(2,1)} async-done(((bf16[128,1152]{1,0:T(8,128)(2,1)}), bf16[32,1152]{1,0:T(8,128)(2,1)}) %reduce-scatter.2.cloned.1.call-update) | async-done | bytes 73744 | tf_op jit(solution)/shard_map/while/body/eval_jaxpr/reduce_scatter | solution.py:64
  398.9 6.8 all_gather.12
  410.9 14.3 %reduce-scatter.2.cloned.1.call-done = bf16[32,1152]{1,0:T(8,128)(2,1)} async-done(((bf16[128,1152]{1,0:T(8,128)(2,1)}), bf16[32,1152]{1,0:T(8,128)(2,1)}) %reduce-scatter.2.cloned.1.call-update) | async-done | bytes 73744 | tf_op jit(solution)/shard_map/while/body/eval_jaxpr/reduce_scatter | solution.py:64
  437.3 6.8 all_gather.12
  449.3 14.3 %reduce-scatter.2.cloned.1.call-done = bf16[32,1152]{1,0:T(8,128)(2,1)} async-done(((bf16[128,1152]{1,0:T(8,128)(2,1)}), bf16[32,1152]{1,0:T(8,128)(2,1)}) %reduce-scatter.2.cloned.1.call-update) | async-done | bytes 73744 | tf_op jit(solution)/shard_map/while/body/eval_jaxpr/reduce_scatter | solution.py:64
  475.6 6.8 all_gather.12
  487.7 14.3 %reduce-scatter.2.cloned.1.call-done = bf16[32,1152]{1,0:T(8,128)(2,1)} async-done(((bf16[128,1152]{1,0:T(8,128)(2,1)}), bf16[32,1152]{1,0:T(8,128)(2,1)}) %reduce-scatter.2.cloned.1.call-update) | async-done | bytes 73744 | tf_op jit(solution)/shard_map/while/body/eval_jaxpr/reduce_scatter | solution.py:64
  514.0 6.8 all_gather.12
  526.0 14.3 %reduce-scatter.2.cloned.1.call-done = bf16[32,1152]{1,0:T(8,128)(2,1)} async-done(((bf16[128,1152]{1,0:T(8,128)(2,1)}), bf16[32,1152]{1,0:T(8,128)(2,1)}) %reduce-scatter.2.cloned.1.call-update) | async-done | bytes 73744 | tf_op jit(solution)/shard_map/while/body/eval_jaxpr/reduce_scatter | solution.py:64
  552.4 6.8 all_gather.12
  564.4 14.3 %reduce-scatter.2.cloned.1.call-done = bf16[32,1152]{1,0:T(8,128)(2,1)} async-done(((bf16[128,1152]{1,0:T(8,128)(2,1)}), bf16[32,1152]{1,0:T(8,128)(2,1)}) %reduce-scatter.2.cloned.1.call-update) | async-done | bytes 73744 | tf_op jit(solution)/shard_map/while/body/eval_jaxpr/reduce_scatter | solution.py:64
  590.8 6.8 all_gather.12
  602.8 14.3 %reduce-scatter.2.cloned.1.call-done = bf16[32,1152]{1,0:T(8,128)(2,1)} async-done(((bf16[128,1152]{1,0:T(8,128)(2,1)}), bf16[32,1152]{1,0:T(8,128)(2,1)}) %reduce-scatter.2.cloned.1.call-update) | async-done | bytes 73744 | tf_op jit(solution)/shard_map/while/body/eval_jaxpr/reduce_scatter | solution.py:64
  629.2 6.8 all_gather.12
  641.2 14.3 %reduce-scatter.2.cloned.1.call-done = bf16[32,1152]{1,0:T(8,128)(2,1)} async-done(((bf16[128,1152]{1,0:T(8,128)(2,1)}), bf16[32,1152]{1,0:T(8,128)(2,1)}) %reduce-scatter.2.cloned.1.call-update) | async-done | bytes 73744 | tf_op jit(solution)/shard_map/while/body/eval_jaxpr/reduce_scatter | solution.py:64
  667.6 6.8 all_gather.12
  679.6 14.3 %reduce-scatter.2.cloned.1.call-done = bf16[32,1152]{1,0:T(8,128)(2,1)} async-done(((bf16[128,1152]{1,0:T(8,128)(2,1)}), bf16[32,1152]{1,0:T(8,128)(2,1)}) %reduce-scatter.2.cloned.1.call-update) | async-done | bytes 73744 | tf_op jit(solution)/shard_map/while/body/eval_jaxpr/reduce_scatter | solution.py:64
  705.9 6.8 all_gather.12
  718.0 14.3 %reduce-scatter.2.cloned.1.call-done = bf16[32,1152]{1,0:T(8,128)(2,1)} async-done(((bf16[128,1152]{1,0:T(8,128)(2,1)}), bf16[32,1152]{1,0:T(8,128)(2,1)}) %reduce-scatter.2.cloned.1.call-update) | async-done | bytes 73744 | tf_op jit(solution)/shard_map/while/body/eval_jaxpr/reduce_scatter | solution.py:64
  744.3 6.8 all_gather.12
  756.3 14.3 %reduce-scatter.2.cloned.1.call-done = bf16[32,1152]{1,0:T(8,128)(2,1)} async-done(((bf16[128,1152]{1,0:T(8,128)(2,1)}), bf16[32,1152]{1,0:T(8,128)(2,1)}) %reduce-scatter.2.cloned.1.call-update) | async-done | bytes 73744 | tf_op jit(solution)/shard_map/while/body/eval_jaxpr/reduce_scatter | solution.py:64
  782.7 6.8 all_gather.12
  794.7 14.3 %reduce-scatter.2.cloned.1.call-done = bf16[32,1152]{1,0:T(8,128)(2,1)} async-done(((bf16[128,1152]{1,0:T(8,128)(2,1)}), bf16[32,1152]{1,0:T(8,128)(2,1)}) %reduce-scatter.2.cloned.1.call-update) | async-done | bytes 73744 | tf_op jit(solution)/shard_map/while/body/eval_jaxpr/reduce_scatter | solution.py:64
  821.1 6.8 all_gather.12
  833.1 14.3 %reduce-scatter.2.cloned.1.call-done = bf16[32,1152]{1,0:T(8,128)(2,1)} async-done(((bf16[128,1152]{1,0:T(8,128)(2,1)}), bf16[32,1152]{1,0:T(8,128)(2,1)}) %reduce-scatter.2.cloned.1.call-update) | async-done | bytes 73744 | tf_op jit(solution)/shard_map/while/body/eval_jaxpr/reduce_scatter | solution.py:64
  859.5 6.8 all_gather.12
  871.5 14.3 %reduce-scatter.2.cloned.1.call-done = bf16[32,1152]{1,0:T(8,128)(2,1)} async-done(((bf16[128,1152]{1,0:T(8,128)(2,1)}), bf16[32,1152]{1,0:T(8,128)(2,1)}) %reduce-scatter.2.cloned.1.call-update) | async-done | bytes 73744 | tf_op jit(solution)/shard_map/while/body/eval_jaxpr/reduce_scatter | solution.py:64
  897.9 6.8 all_gather.12
  909.9 14.3 %reduce-scatter.2.cloned.1.call-done = bf16[32,1152]{1,0:T(8,128)(2,1)} async-done(((bf16[128,1152]{1,0:T(8,128)(2,1)}), bf16[32,1152]{1,0:T(8,128)(2,1)}) %reduce-scatter.2.cloned.1.call-update) | async-done | bytes 73744 | tf_op jit(solution)/shard_map/while/body/eval_jaxpr/reduce_scatter | solution.py:64
  936.2 6.8 all_gather.12
  948.3 14.3 %reduce-scatter.2.cloned.1.call-done = bf16[32,1152]{1,0:T(8,128)(2,1)} async-done(((bf16[128,1152]{1,0:T(8,128)(2,1)}), bf16[32,1152]{1,0:T(8,128)(2,1)}) %reduce-scatter.2.cloned.1.call-update) | async-done | bytes 73744 | tf_op jit(solution)/shard_map/while/body/eval_jaxpr/reduce_scatter | solution.py:64
  974.6 6.8 all_gather.12
  986.6 14.3 %reduce-scatter.2.cloned.1.call-done = bf16[32,1152]{1,0:T(8,128)(2,1)} async-done(((bf16[128,1152]{1,0:T(8,128)(2,1)}), bf16[32,1152]{1,0:T(8,128)(2,1)}) %reduce-scatter.2.cloned.1.call-update) | async-done | bytes 73744 | tf_op jit(solution)/shard_map/while/body/eval_jaxpr/reduce_scatter | solution.py:64
  1013.0 6.8 all_gather.12
  1025.0 14.3 %reduce-scatter.2.cloned.1.call-done = bf16[32,1152]{1,0:T(8,128)(2,1)} async-done(((bf16[128,1152]{1,0:T(8,128)(2,1)}), bf16[32,1152]{1,0:T(8,128)(2,1)}) %reduce-scatter.2.cloned.1.call-update) | async-done | bytes 73744 | tf_op jit(solution)/shard_map/while/body/eval_jaxpr/reduce_scatter | solution.py:64
  1051.4 6.8 all_gather.12
  1063.4 14.3 %reduce-scatter.2.cloned.1.call-done = bf16[32,1152]{1,0:T(8,128)(2,1)} async-done(((bf16[128,1152]{1,0:T(8,128)(2,1)}), bf16[32,1152]{1,0:T(8,128)(2,1)}) %reduce-scatter.2.cloned.1.call-update) | async-done | bytes 73744 | tf_op jit(solution)/shard_map/while/body/eval_jaxpr/reduce_scatter | solution.py:64
  1089.8 6.8 all_gather.12
  1101.8 14.3 %reduce-scatter.2.cloned.1.call-done = bf16[32,1152]{1,0:T(8,128)(2,1)} async-done(((bf16[128,1152]{1,0:T(8,128)(2,1)}), bf16[32,1152]{1,0:T(8,128)(2,1)}) %reduce-scatter.2.cloned.1.call-update) | async-done | bytes 73744 | tf_op jit(solution)/shard_map/while/body/eval_jaxpr/reduce_scatter | solution.py:64
  1128.2 6.8 all_gather.12
  1140.2 14.3 %reduce-scatter.2.cloned.1.call-done = bf16[32,1152]{1,0:T(8,128)(2,1)} async-done(((bf16[128,1152]{1,0:T(8,128)(2,1)}), bf16[32,1152]{1,0:T(8,128)(2,1)}) %reduce-scatter.2.cloned.1.call-update) | async-done | bytes 73744 | tf_op jit(solution)/shard_map/while/body/eval_jaxpr/reduce_scatter | solution.py:64
  1166.5 6.8 all_gather.12
  1178.6 14.3 %reduce-scatter.2.cloned.1.call-done = bf16[32,1152]{1,0:T(8,128)(2,1)} async-done(((bf16[128,1152]{1,0:T(8,128)(2,1)}), bf16[32,1152]{1,0:T(8,128)(2,1)}) %reduce-scatter.2.cloned.1.call-update) | async-done | bytes 73744 | tf_op jit(solution)/shard_map/while/body/eval_jaxpr/reduce_scatter | solution.py:64
  1204.9 6.8 all_gather.12
  1216.9 14.3 %reduce-scatter.2.cloned.1.call-done = bf16[32,1152]{1,0:T(8,128)(2,1)} async-done(((bf16[128,1152]{1,0:T(8,128)(2,1)}), bf16[32,1152]{1,0:T(8,128)(2,1)}) %reduce-scatter.2.cloned.1.call-update) | async-done | bytes 73744 | tf_op jit(solution)/shard_map/while/body/eval_jaxpr/reduce_scatter | solution.py:64
  (453 shorter events, 562.2 us)
Async XLA Ops:
  8.8 32.6 %reduce-scatter.2.cloned.1.call-start = ((), (), s32[]{:S(2)}) async-start(), calls=%async_computation.1 | async-start | bytes 368640 | tf_op jit(solution)/shard_map/while/body/eval_jaxpr/reduce_scatter | solution.py:64
  21.8 26.1 %collective-permute-start = (bf16[32,1152]{1,0:T(8,128)(2,1)S(1)}, bf16[32,1152]{1,0:T(8,128)(2,1)S(1)}, u32[]{:S(2)}, u32[]{:S(2)}) collective-permute-start(bf16[32,1152]{1,0:T(8,128)(2,1)S(1)} %copy.13), channel_id=1, source_target_pairs={{0,4},{4,8},{8,12},{12,16},{16,20},{20,24},{24,28},{28,32},{32,36}... | collective-permute-start | bytes 221192 | tf_op jit(solution)/shard_map/while/body/eval_jaxpr/ppermute | solution.py:9
  53.5 26.3 %reduce-scatter.2.cloned.1.call-start = ((), (), s32[]{:S(2)}) async-start(), calls=%async_computation.1 | async-start | bytes 368640 | tf_op jit(solution)/shard_map/while/body/eval_jaxpr/reduce_scatter | solution.py:64
  65.4 24.2 %collective-permute-start = (bf16[32,1152]{1,0:T(8,128)(2,1)S(1)}, bf16[32,1152]{1,0:T(8,128)(2,1)S(1)}, u32[]{:S(2)}, u32[]{:S(2)}) collective-permute-start(bf16[32,1152]{1,0:T(8,128)(2,1)S(1)} %copy.13), channel_id=1, source_target_pairs={{0,4},{4,8},{8,12},{12,16},{16,20},{20,24},{24,28},{28,32},{32,36}... | collective-permute-start | bytes 221192 | tf_op jit(solution)/shard_map/while/body/eval_jaxpr/ppermute | solution.py:9
  91.8 26.3 %reduce-scatter.2.cloned.1.call-start = ((), (), s32[]{:S(2)}) async-start(), calls=%async_computation.1 | async-start | bytes 368640 | tf_op jit(solution)/shard_map/while/body/eval_jaxpr/reduce_scatter | solution.py:64
  103.8 24.2 %collective-permute-start = (bf16[32,1152]{1,0:T(8,128)(2,1)S(1)}, bf16[32,1152]{1,0:T(8,128)(2,1)S(1)}, u32[]{:S(2)}, u32[]{:S(2)}) collective-permute-start(bf16[32,1152]{1,0:T(8,128)(2,1)S(1)} %copy.13), channel_id=1, source_target_pairs={{0,4},{4,8},{8,12},{12,16},{16,20},{20,24},{24,28},{28,32},{32,36}... | collective-permute-start | bytes 221192 | tf_op jit(solution)/shard_map/while/body/eval_jaxpr/ppermute | solution.py:9
  130.2 26.4 %reduce-scatter.2.cloned.1.call-start = ((), (), s32[]{:S(2)}) async-start(), calls=%async_computation.1 | async-start | bytes 368640 | tf_op jit(solution)/shard_map/while/body/eval_jaxpr/reduce_scatter | solution.py:64
  142.1 24.2 %collective-permute-start = (bf16[32,1152]{1,0:T(8,128)(2,1)S(1)}, bf16[32,1152]{1,0:T(8,128)(2,1)S(1)}, u32[]{:S(2)}, u32[]{:S(2)}) collective-permute-start(bf16[32,1152]{1,0:T(8,128)(2,1)S(1)} %copy.13), channel_id=1, source_target_pairs={{0,4},{4,8},{8,12},{12,16},{16,20},{20,24},{24,28},{28,32},{32,36}... | collective-permute-start | bytes 221192 | tf_op jit(solution)/shard_map/while/body/eval_jaxpr/ppermute | solution.py:9
  168.6 26.3 %reduce-scatter.2.cloned.1.call-start = ((), (), s32[]{:S(2)}) async-start(), calls=%async_computation.1 | async-start | bytes 368640 | tf_op jit(solution)/shard_map/while/body/eval_jaxpr/reduce_scatter | solution.py:64
  180.5 24.2 %collective-permute-start = (bf16[32,1152]{1,0:T(8,128)(2,1)S(1)}, bf16[32,1152]{1,0:T(8,128)(2,1)S(1)}, u32[]{:S(2)}, u32[]{:S(2)}) collective-permute-start(bf16[32,1152]{1,0:T(8,128)(2,1)S(1)} %copy.13), channel_id=1, source_target_pairs={{0,4},{4,8},{8,12},{12,16},{16,20},{20,24},{24,28},{28,32},{32,36}... | collective-permute-start | bytes 221192 | tf_op jit(solution)/shard_map/while/body/eval_jaxpr/ppermute | solution.py:9
  206.9 26.4 %reduce-scatter.2.cloned.1.call-start = ((), (), s32[]{:S(2)}) async-start(), calls=%async_computation.1 | async-start | bytes 368640 | tf_op jit(solution)/shard_map/while/body/eval_jaxpr/reduce_scatter | solution.py:64
  218.9 24.2 %collective-permute-start = (bf16[32,1152]{1,0:T(8,128)(2,1)S(1)}, bf16[32,1152]{1,0:T(8,128)(2,1)S(1)}, u32[]{:S(2)}, u32[]{:S(2)}) collective-permute-start(bf16[32,1152]{1,0:T(8,128)(2,1)S(1)} %copy.13), channel_id=1, source_target_pairs={{0,4},{4,8},{8,12},{12,16},{16,20},{20,24},{24,28},{28,32},{32,36}... | collective-permute-start | bytes 221192 | tf_op jit(solution)/shard_map/while/body/eval_jaxpr/ppermute | solution.py:9
  245.3 26.4 %reduce-scatter.2.cloned.1.call-start = ((), (), s32[]{:S(2)}) async-start(), calls=%async_computation.1 | async-start | bytes 368640 | tf_op jit(solution)/shard_map/while/body/eval_jaxpr/reduce_scatter | solution.py:64
  257.3 24.2 %collective-permute-start = (bf16[32,1152]{1,0:T(8,128)(2,1)S(1)}, bf16[32,1152]{1,0:T(8,128)(2,1)S(1)}, u32[]{:S(2)}, u32[]{:S(2)}) collective-permute-start(bf16[32,1152]{1,0:T(8,128)(2,1)S(1)} %copy.13), channel_id=1, source_target_pairs={{0,4},{4,8},{8,12},{12,16},{16,20},{20,24},{24,28},{28,32},{32,36}... | collective-permute-start | bytes 221192 | tf_op jit(solution)/shard_map/while/body/eval_jaxpr/ppermute | solution.py:9
  283.7 26.4 %reduce-scatter.2.cloned.1.call-start = ((), (), s32[]{:S(2)}) async-start(), calls=%async_computation.1 | async-start | bytes 368640 | tf_op jit(solution)/shard_map/while/body/eval_jaxpr/reduce_scatter | solution.py:64
  295.7 24.2 %collective-permute-start = (bf16[32,1152]{1,0:T(8,128)(2,1)S(1)}, bf16[32,1152]{1,0:T(8,128)(2,1)S(1)}, u32[]{:S(2)}, u32[]{:S(2)}) collective-permute-start(bf16[32,1152]{1,0:T(8,128)(2,1)S(1)} %copy.13), channel_id=1, source_target_pairs={{0,4},{4,8},{8,12},{12,16},{16,20},{20,24},{24,28},{28,32},{32,36}... | collective-permute-start | bytes 221192 | tf_op jit(solution)/shard_map/while/body/eval_jaxpr/ppermute | solution.py:9
  322.1 26.4 %reduce-scatter.2.cloned.1.call-start = ((), (), s32[]{:S(2)}) async-start(), calls=%async_computation.1 | async-start | bytes 368640 | tf_op jit(solution)/shard_map/while/body/eval_jaxpr/reduce_scatter | solution.py:64
  334.0 24.2 %collective-permute-start = (bf16[32,1152]{1,0:T(8,128)(2,1)S(1)}, bf16[32,1152]{1,0:T(8,128)(2,1)S(1)}, u32[]{:S(2)}, u32[]{:S(2)}) collective-permute-start(bf16[32,1152]{1,0:T(8,128)(2,1)S(1)} %copy.13), channel_id=1, source_target_pairs={{0,4},{4,8},{8,12},{12,16},{16,20},{20,24},{24,28},{28,32},{32,36}... | collective-permute-start | bytes 221192 | tf_op jit(solution)/shard_map/while/body/eval_jaxpr/ppermute | solution.py:9
  360.5 26.4 %reduce-scatter.2.cloned.1.call-start = ((), (), s32[]{:S(2)}) async-start(), calls=%async_computation.1 | async-start | bytes 368640 | tf_op jit(solution)/shard_map/while/body/eval_jaxpr/reduce_scatter | solution.py:64
  372.4 24.2 %collective-permute-start = (bf16[32,1152]{1,0:T(8,128)(2,1)S(1)}, bf16[32,1152]{1,0:T(8,128)(2,1)S(1)}, u32[]{:S(2)}, u32[]{:S(2)}) collective-permute-start(bf16[32,1152]{1,0:T(8,128)(2,1)S(1)} %copy.13), channel_id=1, source_target_pairs={{0,4},{4,8},{8,12},{12,16},{16,20},{20,24},{24,28},{28,32},{32,36}... | collective-permute-start | bytes 221192 | tf_op jit(solution)/shard_map/while/body/eval_jaxpr/ppermute | solution.py:9
  398.9 26.4 %reduce-scatter.2.cloned.1.call-start = ((), (), s32[]{:S(2)}) async-start(), calls=%async_computation.1 | async-start | bytes 368640 | tf_op jit(solution)/shard_map/while/body/eval_jaxpr/reduce_scatter | solution.py:64
  410.8 24.2 %collective-permute-start = (bf16[32,1152]{1,0:T(8,128)(2,1)S(1)}, bf16[32,1152]{1,0:T(8,128)(2,1)S(1)}, u32[]{:S(2)}, u32[]{:S(2)}) collective-permute-start(bf16[32,1152]{1,0:T(8,128)(2,1)S(1)} %copy.13), channel_id=1, source_target_pairs={{0,4},{4,8},{8,12},{12,16},{16,20},{20,24},{24,28},{28,32},{32,36}... | collective-permute-start | bytes 221192 | tf_op jit(solution)/shard_map/while/body/eval_jaxpr/ppermute | solution.py:9
  437.2 26.4 %reduce-scatter.2.cloned.1.call-start = ((), (), s32[]{:S(2)}) async-start(), calls=%async_computation.1 | async-start | bytes 368640 | tf_op jit(solution)/shard_map/while/body/eval_jaxpr/reduce_scatter | solution.py:64
  449.2 24.2 %collective-permute-start = (bf16[32,1152]{1,0:T(8,128)(2,1)S(1)}, bf16[32,1152]{1,0:T(8,128)(2,1)S(1)}, u32[]{:S(2)}, u32[]{:S(2)}) collective-permute-start(bf16[32,1152]{1,0:T(8,128)(2,1)S(1)} %copy.13), channel_id=1, source_target_pairs={{0,4},{4,8},{8,12},{12,16},{16,20},{20,24},{24,28},{28,32},{32,36}... | collective-permute-start | bytes 221192 | tf_op jit(solution)/shard_map/while/body/eval_jaxpr/ppermute | solution.py:9
  475.6 26.4 %reduce-scatter.2.cloned.1.call-start = ((), (), s32[]{:S(2)}) async-start(), calls=%async_computation.1 | async-start | bytes 368640 | tf_op jit(solution)/shard_map/while/body/eval_jaxpr/reduce_scatter | solution.py:64
  487.6 24.2 %collective-permute-start = (bf16[32,1152]{1,0:T(8,128)(2,1)S(1)}, bf16[32,1152]{1,0:T(8,128)(2,1)S(1)}, u32[]{:S(2)}, u32[]{:S(2)}) collective-permute-start(bf16[32,1152]{1,0:T(8,128)(2,1)S(1)} %copy.13), channel_id=1, source_target_pairs={{0,4},{4,8},{8,12},{12,16},{16,20},{20,24},{24,28},{28,32},{32,36}... | collective-permute-start | bytes 221192 | tf_op jit(solution)/shard_map/while/body/eval_jaxpr/ppermute | solution.py:9
  514.0 26.4 %reduce-scatter.2.cloned.1.call-start = ((), (), s32[]{:S(2)}) async-start(), calls=%async_computation.1 | async-start | bytes 368640 | tf_op jit(solution)/shard_map/while/body/eval_jaxpr/reduce_scatter | solution.py:64
  526.0 24.2 %collective-permute-start = (bf16[32,1152]{1,0:T(8,128)(2,1)S(1)}, bf16[32,1152]{1,0:T(8,128)(2,1)S(1)}, u32[]{:S(2)}, u32[]{:S(2)}) collective-permute-start(bf16[32,1152]{1,0:T(8,128)(2,1)S(1)} %copy.13), channel_id=1, source_target_pairs={{0,4},{4,8},{8,12},{12,16},{16,20},{20,24},{24,28},{28,32},{32,36}... | collective-permute-start | bytes 221192 | tf_op jit(solution)/shard_map/while/body/eval_jaxpr/ppermute | solution.py:9
  552.4 26.4 %reduce-scatter.2.cloned.1.call-start = ((), (), s32[]{:S(2)}) async-start(), calls=%async_computation.1 | async-start | bytes 368640 | tf_op jit(solution)/shard_map/while/body/eval_jaxpr/reduce_scatter | solution.py:64
  564.3 24.2 %collective-permute-start = (bf16[32,1152]{1,0:T(8,128)(2,1)S(1)}, bf16[32,1152]{1,0:T(8,128)(2,1)S(1)}, u32[]{:S(2)}, u32[]{:S(2)}) collective-permute-start(bf16[32,1152]{1,0:T(8,128)(2,1)S(1)} %copy.13), channel_id=1, source_target_pairs={{0,4},{4,8},{8,12},{12,16},{16,20},{20,24},{24,28},{28,32},{32,36}... | collective-permute-start | bytes 221192 | tf_op jit(solution)/shard_map/while/body/eval_jaxpr/ppermute | solution.py:9
  590.8 26.4 %reduce-scatter.2.cloned.1.call-start = ((), (), s32[]{:S(2)}) async-start(), calls=%async_computation.1 | async-start | bytes 368640 | tf_op jit(solution)/shard_map/while/body/eval_jaxpr/reduce_scatter | solution.py:64
  602.7 24.2 %collective-permute-start = (bf16[32,1152]{1,0:T(8,128)(2,1)S(1)}, bf16[32,1152]{1,0:T(8,128)(2,1)S(1)}, u32[]{:S(2)}, u32[]{:S(2)}) collective-permute-start(bf16[32,1152]{1,0:T(8,128)(2,1)S(1)} %copy.13), channel_id=1, source_target_pairs={{0,4},{4,8},{8,12},{12,16},{16,20},{20,24},{24,28},{28,32},{32,36}... | collective-permute-start | bytes 221192 | tf_op jit(solution)/shard_map/while/body/eval_jaxpr/ppermute | solution.py:9
  629.1 26.4 %reduce-scatter.2.cloned.1.call-start = ((), (), s32[]{:S(2)}) async-start(), calls=%async_computation.1 | async-start | bytes 368640 | tf_op jit(solution)/shard_map/while/body/eval_jaxpr/reduce_scatter | solution.py:64
  641.1 24.2 %collective-permute-start = (bf16[32,1152]{1,0:T(8,128)(2,1)S(1)}, bf16[32,1152]{1,0:T(8,128)(2,1)S(1)}, u32[]{:S(2)}, u32[]{:S(2)}) collective-permute-start(bf16[32,1152]{1,0:T(8,128)(2,1)S(1)} %copy.13), channel_id=1, source_target_pairs={{0,4},{4,8},{8,12},{12,16},{16,20},{20,24},{24,28},{28,32},{32,36}... | collective-permute-start | bytes 221192 | tf_op jit(solution)/shard_map/while/body/eval_jaxpr/ppermute | solution.py:9
  667.5 26.4 %reduce-scatter.2.cloned.1.call-start = ((), (), s32[]{:S(2)}) async-start(), calls=%async_computation.1 | async-start | bytes 368640 | tf_op jit(solution)/shard_map/while/body/eval_jaxpr/reduce_scatter | solution.py:64
  679.5 24.2 %collective-permute-start = (bf16[32,1152]{1,0:T(8,128)(2,1)S(1)}, bf16[32,1152]{1,0:T(8,128)(2,1)S(1)}, u32[]{:S(2)}, u32[]{:S(2)}) collective-permute-start(bf16[32,1152]{1,0:T(8,128)(2,1)S(1)} %copy.13), channel_id=1, source_target_pairs={{0,4},{4,8},{8,12},{12,16},{16,20},{20,24},{24,28},{28,32},{32,36}... | collective-permute-start | bytes 221192 | tf_op jit(solution)/shard_map/while/body/eval_jaxpr/ppermute | solution.py:9
  705.9 26.4 %reduce-scatter.2.cloned.1.call-start = ((), (), s32[]{:S(2)}) async-start(), calls=%async_computation.1 | async-start | bytes 368640 | tf_op jit(solution)/shard_map/while/body/eval_jaxpr/reduce_scatter | solution.py:64
  717.9 24.2 %collective-permute-start = (bf16[32,1152]{1,0:T(8,128)(2,1)S(1)}, bf16[32,1152]{1,0:T(8,128)(2,1)S(1)}, u32[]{:S(2)}, u32[]{:S(2)}) collective-permute-start(bf16[32,1152]{1,0:T(8,128)(2,1)S(1)} %copy.13), channel_id=1, source_target_pairs={{0,4},{4,8},{8,12},{12,16},{16,20},{20,24},{24,28},{28,32},{32,36}... | collective-permute-start | bytes 221192 | tf_op jit(solution)/shard_map/while/body/eval_jaxpr/ppermute | solution.py:9
  744.3 26.4 %reduce-scatter.2.cloned.1.call-start = ((), (), s32[]{:S(2)}) async-start(), calls=%async_computation.1 | async-start | bytes 368640 | tf_op jit(solution)/shard_map/while/body/eval_jaxpr/reduce_scatter | solution.py:64
  756.2 24.2 %collective-permute-start = (bf16[32,1152]{1,0:T(8,128)(2,1)S(1)}, bf16[32,1152]{1,0:T(8,128)(2,1)S(1)}, u32[]{:S(2)}, u32[]{:S(2)}) collective-permute-start(bf16[32,1152]{1,0:T(8,128)(2,1)S(1)} %copy.13), channel_id=1, source_target_pairs={{0,4},{4,8},{8,12},{12,16},{16,20},{20,24},{24,28},{28,32},{32,36}... | collective-permute-start | bytes 221192 | tf_op jit(solution)/shard_map/while/body/eval_jaxpr/ppermute | solution.py:9
  782.7 26.4 %reduce-scatter.2.cloned.1.call-start = ((), (), s32[]{:S(2)}) async-start(), calls=%async_computation.1 | async-start | bytes 368640 | tf_op jit(solution)/shard_map/while/body/eval_jaxpr/reduce_scatter | solution.py:64
  794.6 24.2 %collective-permute-start = (bf16[32,1152]{1,0:T(8,128)(2,1)S(1)}, bf16[32,1152]{1,0:T(8,128)(2,1)S(1)}, u32[]{:S(2)}, u32[]{:S(2)}) collective-permute-start(bf16[32,1152]{1,0:T(8,128)(2,1)S(1)} %copy.13), channel_id=1, source_target_pairs={{0,4},{4,8},{8,12},{12,16},{16,20},{20,24},{24,28},{28,32},{32,36}... | collective-permute-start | bytes 221192 | tf_op jit(solution)/shard_map/while/body/eval_jaxpr/ppermute | solution.py:9
  821.1 26.4 %reduce-scatter.2.cloned.1.call-start = ((), (), s32[]{:S(2)}) async-start(), calls=%async_computation.1 | async-start | bytes 368640 | tf_op jit(solution)/shard_map/while/body/eval_jaxpr/reduce_scatter | solution.py:64
  833.0 24.2 %collective-permute-start = (bf16[32,1152]{1,0:T(8,128)(2,1)S(1)}, bf16[32,1152]{1,0:T(8,128)(2,1)S(1)}, u32[]{:S(2)}, u32[]{:S(2)}) collective-permute-start(bf16[32,1152]{1,0:T(8,128)(2,1)S(1)} %copy.13), channel_id=1, source_target_pairs={{0,4},{4,8},{8,12},{12,16},{16,20},{20,24},{24,28},{28,32},{32,36}... | collective-permute-start | bytes 221192 | tf_op jit(solution)/shard_map/while/body/eval_jaxpr/ppermute | solution.py:9
  859.4 26.4 %reduce-scatter.2.cloned.1.call-start = ((), (), s32[]{:S(2)}) async-start(), calls=%async_computation.1 | async-start | bytes 368640 | tf_op jit(solution)/shard_map/while/body/eval_jaxpr/reduce_scatter | solution.py:64
  871.4 24.2 %collective-permute-start = (bf16[32,1152]{1,0:T(8,128)(2,1)S(1)}, bf16[32,1152]{1,0:T(8,128)(2,1)S(1)}, u32[]{:S(2)}, u32[]{:S(2)}) collective-permute-start(bf16[32,1152]{1,0:T(8,128)(2,1)S(1)} %copy.13), channel_id=1, source_target_pairs={{0,4},{4,8},{8,12},{12,16},{16,20},{20,24},{24,28},{28,32},{32,36}... | collective-permute-start | bytes 221192 | tf_op jit(solution)/shard_map/while/body/eval_jaxpr/ppermute | solution.py:9
  897.8 26.4 %reduce-scatter.2.cloned.1.call-start = ((), (), s32[]{:S(2)}) async-start(), calls=%async_computation.1 | async-start | bytes 368640 | tf_op jit(solution)/shard_map/while/body/eval_jaxpr/reduce_scatter | solution.py:64
  909.8 24.2 %collective-permute-start = (bf16[32,1152]{1,0:T(8,128)(2,1)S(1)}, bf16[32,1152]{1,0:T(8,128)(2,1)S(1)}, u32[]{:S(2)}, u32[]{:S(2)}) collective-permute-start(bf16[32,1152]{1,0:T(8,128)(2,1)S(1)} %copy.13), channel_id=1, source_target_pairs={{0,4},{4,8},{8,12},{12,16},{16,20},{20,24},{24,28},{28,32},{32,36}... | collective-permute-start | bytes 221192 | tf_op jit(solution)/shard_map/while/body/eval_jaxpr/ppermute | solution.py:9
  936.2 26.4 %reduce-scatter.2.cloned.1.call-start = ((), (), s32[]{:S(2)}) async-start(), calls=%async_computation.1 | async-start | bytes 368640 | tf_op jit(solution)/shard_map/while/body/eval_jaxpr/reduce_scatter | solution.py:64
  948.2 24.2 %collective-permute-start = (bf16[32,1152]{1,0:T(8,128)(2,1)S(1)}, bf16[32,1152]{1,0:T(8,128)(2,1)S(1)}, u32[]{:S(2)}, u32[]{:S(2)}) collective-permute-start(bf16[32,1152]{1,0:T(8,128)(2,1)S(1)} %copy.13), channel_id=1, source_target_pairs={{0,4},{4,8},{8,12},{12,16},{16,20},{20,24},{24,28},{28,32},{32,36}... | collective-permute-start | bytes 221192 | tf_op jit(solution)/shard_map/while/body/eval_jaxpr/ppermute | solution.py:9
  974.6 26.4 %reduce-scatter.2.cloned.1.call-start = ((), (), s32[]{:S(2)}) async-start(), calls=%async_computation.1 | async-start | bytes 368640 | tf_op jit(solution)/shard_map/while/body/eval_jaxpr/reduce_scatter | solution.py:64
  986.5 24.2 %collective-permute-start = (bf16[32,1152]{1,0:T(8,128)(2,1)S(1)}, bf16[32,1152]{1,0:T(8,128)(2,1)S(1)}, u32[]{:S(2)}, u32[]{:S(2)}) collective-permute-start(bf16[32,1152]{1,0:T(8,128)(2,1)S(1)} %copy.13), channel_id=1, source_target_pairs={{0,4},{4,8},{8,12},{12,16},{16,20},{20,24},{24,28},{28,32},{32,36}... | collective-permute-start | bytes 221192 | tf_op jit(solution)/shard_map/while/body/eval_jaxpr/ppermute | solution.py:9
  1013.0 26.4 %reduce-scatter.2.cloned.1.call-start = ((), (), s32[]{:S(2)}) async-start(), calls=%async_computation.1 | async-start | bytes 368640 | tf_op jit(solution)/shard_map/while/body/eval_jaxpr/reduce_scatter | solution.py:64
  1024.9 24.2 %collective-permute-start = (bf16[32,1152]{1,0:T(8,128)(2,1)S(1)}, bf16[32,1152]{1,0:T(8,128)(2,1)S(1)}, u32[]{:S(2)}, u32[]{:S(2)}) collective-permute-start(bf16[32,1152]{1,0:T(8,128)(2,1)S(1)} %copy.13), channel_id=1, source_target_pairs={{0,4},{4,8},{8,12},{12,16},{16,20},{20,24},{24,28},{28,32},{32,36}... | collective-permute-start | bytes 221192 | tf_op jit(solution)/shard_map/while/body/eval_jaxpr/ppermute | solution.py:9
  1051.4 26.4 %reduce-scatter.2.cloned.1.call-start = ((), (), s32[]{:S(2)}) async-start(), calls=%async_computation.1 | async-start | bytes 368640 | tf_op jit(solution)/shard_map/while/body/eval_jaxpr/reduce_scatter | solution.py:64
  1063.3 24.2 %collective-permute-start = (bf16[32,1152]{1,0:T(8,128)(2,1)S(1)}, bf16[32,1152]{1,0:T(8,128)(2,1)S(1)}, u32[]{:S(2)}, u32[]{:S(2)}) collective-permute-start(bf16[32,1152]{1,0:T(8,128)(2,1)S(1)} %copy.13), channel_id=1, source_target_pairs={{0,4},{4,8},{8,12},{12,16},{16,20},{20,24},{24,28},{28,32},{32,36}... | collective-permute-start | bytes 221192 | tf_op jit(solution)/shard_map/while/body/eval_jaxpr/ppermute | solution.py:9
  1089.7 26.4 %reduce-scatter.2.cloned.1.call-start = ((), (), s32[]{:S(2)}) async-start(), calls=%async_computation.1 | async-start | bytes 368640 | tf_op jit(solution)/shard_map/while/body/eval_jaxpr/reduce_scatter | solution.py:64
  1101.7 24.2 %collective-permute-start = (bf16[32,1152]{1,0:T(8,128)(2,1)S(1)}, bf16[32,1152]{1,0:T(8,128)(2,1)S(1)}, u32[]{:S(2)}, u32[]{:S(2)}) collective-permute-start(bf16[32,1152]{1,0:T(8,128)(2,1)S(1)} %copy.13), channel_id=1, source_target_pairs={{0,4},{4,8},{8,12},{12,16},{16,20},{20,24},{24,28},{28,32},{32,36}... | collective-permute-start | bytes 221192 | tf_op jit(solution)/shard_map/while/body/eval_jaxpr/ppermute | solution.py:9
  1128.1 26.4 %reduce-scatter.2.cloned.1.call-start = ((), (), s32[]{:S(2)}) async-start(), calls=%async_computation.1 | async-start | bytes 368640 | tf_op jit(solution)/shard_map/while/body/eval_jaxpr/reduce_scatter | solution.py:64
  1140.1 24.2 %collective-permute-start = (bf16[32,1152]{1,0:T(8,128)(2,1)S(1)}, bf16[32,1152]{1,0:T(8,128)(2,1)S(1)}, u32[]{:S(2)}, u32[]{:S(2)}) collective-permute-start(bf16[32,1152]{1,0:T(8,128)(2,1)S(1)} %copy.13), channel_id=1, source_target_pairs={{0,4},{4,8},{8,12},{12,16},{16,20},{20,24},{24,28},{28,32},{32,36}... | collective-permute-start | bytes 221192 | tf_op jit(solution)/shard_map/while/body/eval_jaxpr/ppermute | solution.py:9
  1166.5 26.4 %reduce-scatter.2.cloned.1.call-start = ((), (), s32[]{:S(2)}) async-start(), calls=%async_computation.1 | async-start | bytes 368640 | tf_op jit(solution)/shard_map/while/body/eval_jaxpr/reduce_scatter | solution.py:64
  1178.5 24.2 %collective-permute-start = (bf16[32,1152]{1,0:T(8,128)(2,1)S(1)}, bf16[32,1152]{1,0:T(8,128)(2,1)S(1)}, u32[]{:S(2)}, u32[]{:S(2)}) collective-permute-start(bf16[32,1152]{1,0:T(8,128)(2,1)S(1)} %copy.13), channel_id=1, source_target_pairs={{0,4},{4,8},{8,12},{12,16},{16,20},{20,24},{24,28},{28,32},{32,36}... | collective-permute-start | bytes 221192 | tf_op jit(solution)/shard_map/while/body/eval_jaxpr/ppermute | solution.py:9
  1204.9 26.4 %reduce-scatter.2.cloned.1.call-start = ((), (), s32[]{:S(2)}) async-start(), calls=%async_computation.1 | async-start | bytes 368640 | tf_op jit(solution)/shard_map/while/body/eval_jaxpr/reduce_scatter | solution.py:64
  1216.8 24.2 %collective-permute-start = (bf16[32,1152]{1,0:T(8,128)(2,1)S(1)}, bf16[32,1152]{1,0:T(8,128)(2,1)S(1)}, u32[]{:S(2)}, u32[]{:S(2)}) collective-permute-start(bf16[32,1152]{1,0:T(8,128)(2,1)S(1)} %copy.13), channel_id=1, source_target_pairs={{0,4},{4,8},{8,12},{12,16},{16,20},{20,24},{24,28},{28,32},{32,36}... | collective-permute-start | bytes 221192 | tf_op jit(solution)/shard_map/while/body/eval_jaxpr/ppermute | solution.py:9
  (64 other events, 697.9 us)
Sparse Core Ops, SparseCore 0:
  21.9 19.4 reduce-scatter.1
  65.5 14.2 reduce-scatter.1
  103.9 14.2 reduce-scatter.1
  142.3 14.2 reduce-scatter.1
  180.6 14.2 reduce-scatter.1
  219.0 14.2 reduce-scatter.1
  257.4 14.2 reduce-scatter.1
  295.8 14.2 reduce-scatter.1
  334.2 14.2 reduce-scatter.1
  372.5 14.2 reduce-scatter.1
  410.9 14.2 reduce-scatter.1
  449.3 14.2 reduce-scatter.1
  487.7 14.2 reduce-scatter.1
  526.1 14.2 reduce-scatter.1
  564.5 14.2 reduce-scatter.1
  602.8 14.2 reduce-scatter.1
  641.2 14.2 reduce-scatter.1
  679.6 14.2 reduce-scatter.1
  718.0 14.2 reduce-scatter.1
  756.4 14.2 reduce-scatter.1
  794.8 14.2 reduce-scatter.1
  833.1 14.2 reduce-scatter.1
  871.5 14.2 reduce-scatter.1
  909.9 14.2 reduce-scatter.1
  948.3 14.2 reduce-scatter.1
  986.7 14.2 reduce-scatter.1
  1025.1 14.2 reduce-scatter.1
  1063.4 14.2 reduce-scatter.1
  1101.8 14.2 reduce-scatter.1
  1140.2 14.2 reduce-scatter.1
  1178.6 14.2 reduce-scatter.1
  1217.0 14.2 reduce-scatter.1
where the time goes:
time: 1260 us; the launch traced here: 1250 us
  waiting for transfers between devices  535 us (42%)
  matrix products  330 us (26%)
  blocking collectives  218 us (17%)
  starting transfers between devices  120 us (10%)
  other arithmetic  28.9 us (2%)
  between operations  14.4 us (1%)
    reduce_scatter x32, waiting for transfers between devices, step(): lax.psum_scatter(returned_grad_part.astype(jnp.bfloat16), 'blk', scatter_...  460 us
    all_gather x32, blocking collectives, step(): joined_tiles = lax.all_gather(tile_length, 'blk', axis=0, tiled=True)  218 us
    dot_general x32, matrix products, both_grads(): jnp.dot(loss_grid_scaled, tile_length, preferred_element_type=jnp.float32)  167 us
    dot_general x32, matrix products, remaining_factors(): lax.dot_general(visual_features, tile_length, (((1,), (1,)), ((), ())), p...  123 us
    ppermute x64, starting transfers between devices, passed_along(): lax.ppermute(array, axis, [(i, (i + by) % peers) for i in range(peers)])  120 us
    ppermute x64, waiting for transfers between devices, passed_along(): lax.ppermute(array, axis, [(i, (i + by) % peers) for i in range(peers)])  74.3 us
    dot_general x32, matrix products, both_grads(): lax.dot_general(loss_grid_scaled, visual_features, (((0,), (0,)), ((), ()...  40.1 us
    add x32, other arithmetic, step(): held + lax.psum_scatter(returned_grad_part.astype(jnp.bfloat16), 'blk', s...  28.8 us
  transfers between devices with their start and end apart: 96, of which 64 were waited for; matrix products, arithmetic and copies ran while one was open for 16% of the time, Pallas kernels for 0%

commit v1 on v0

--- a/solution.py
+++ b/solution.py
@@ -48,7 +48,9 @@
     def step(turn, carry):
         grad_img, tile_length, held = carry
         reference_offset = (wpos - turn) % n_wide
-        joined_tiles = lax.all_gather(tile_length, "blk", axis=0, tiled=True)
+        joined_tiles = jnp.concatenate(
+            lax.all_to_all(jnp.stack([tile_length] * lax.axis_size("blk")), "blk", 0, 0), axis=0
+        )
         loss_grid_scaled = remaining_factors(
             visual_features,
             joined_tiles,

time: 1260 us -> 1400 us (1.11)
  blocking collectives: 218 us -> 0 us
  waiting for transfers between devices: 535 us -> 747 us
  starting transfers between devices: 120 us -> 252 us
  local copies, waits for them, and re-layouts: 1.91 us -> 25.1 us
    all_gather x32 -> x0, blocking collectives: 218 us -> none  [step(): joined_tiles = lax.all_gather(tile_length, 'blk', axis=0, tiled=True)]
    all_to_all x0 -> x32, waiting for transfers between devices: none -> 177 us  [step(): lax.all_to_all(jnp.stack([tile_length] * lax.axis_size('blk')), 'blk', 0, 0)]
    all_to_all x0 -> x32, starting transfers between devices: none -> 144 us  [step(): lax.all_to_all(jnp.stack([tile_length] * lax.axis_size('blk')), 'blk', 0, 0)]
    another operation x0 -> x32, local copies, waits for them, and re-layouts: none -> 23.2 us  [step(): jnp.stack([tile_length] * lax.axis_size('blk'))]
    reduce_scatter x32, waiting for transfers between devices: 460 us -> 482 us  [step(): lax.psum_scatter(returned_grad_part.astype(jnp.bfloat16), 'blk', scatter_...]
  transfers between devices with their start and end apart: 96 -> 128, of which waited for: 64 -> 96; matrix products, arithmetic and copies ran while one was open for 16% -> 14% of each run, Pallas kernels for 0% -> 0%
where the time goes in v1:
time: 1400 us
  waiting for transfers between devices  747 us (53%)
  matrix products  329 us (24%)
  starting transfers between devices  252 us (18%)
  other arithmetic  28.9 us (2%)
  local copies, waits for them, and re-layouts  25.1 us (2%)
  between operations  14.4 us (1%)
    reduce_scatter x32, waiting for transfers between devices, step(): lax.psum_scatter(returned_grad_part.astype(jnp.bfloat16), 'blk', scatter_...  482 us
    all_to_all x32, waiting for transfers between devices, step(): lax.all_to_all(jnp.stack([tile_length] * lax.axis_size('blk')), 'blk', 0, 0)  177 us
    dot_general x32, matrix products, both_grads(): jnp.dot(loss_grid_scaled, tile_length, preferred_element_type=jnp.float32)  167 us
    all_to_all x32, starting transfers between devices, step(): lax.all_to_all(jnp.stack([tile_length] * lax.axis_size('blk')), 'blk', 0, 0)  144 us
    dot_general x32, matrix products, remaining_factors(): lax.dot_general(visual_features, tile_length, (((1,), (1,)), ((), ())), p...  123 us
    ppermute x64, starting transfers between devices, passed_along(): lax.ppermute(array, axis, [(i, (i + by) % peers) for i in range(peers)])  108 us
    ppermute x64, waiting for transfers between devices, passed_along(): lax.ppermute(array, axis, [(i, (i + by) % peers) for i in range(peers)])  88 us
    dot_general x32, matrix products, both_grads(): lax.dot_general(loss_grid_scaled, visual_features, (((0,), (0,)), ((), ()...  39.9 us
  transfers between devices with their start and end apart: 128, of which 96 were waited for; matrix products, arithmetic and copies ran while one was open for 14% of the time, Pallas kernels for 0%

profile of v1, /device:TPU:1, one launch (start us, length us, event | category | flops | bytes accessed | tf_op | source)
XLA Modules:
  0.0 1397.9 jit_solution(13251434701911759520)
XLA Ops:
  8.7 1382.0 %while.20 = (s32[]{:T(128)}, f32[1024,1152]{1,0:T(8,128)}, bf16[32,1152]{1,0:T(8,128)(2,1)S(1)}, f32[32,1152]{1,0:T(8,128)S(1)}, f32[]{:T(128)}, /*index=5*/s32[...) while((s32[]{:T(128)}, f32[1024,1152]{1,0:T(8,128)}, ...), condition=%wide.region_2.3_spmd.clone, body=%wide.region_0.2_spmd.clone.sunk | while | flops 910123136 | bytes 29029856 | solution.py:74
  14.5 5.5 all-to-all-done
  28.9 16.9 %reduce-scatter.2.cloned.1.call-done = bf16[32,1152]{1,0:T(8,128)(2,1)} async-done(((bf16[128,1152]{1,0:T(8,128)(2,1)}), bf16[32,1152]{1,0:T(8,128)(2,1)}) %reduce-scatter.2.cloned.1.call-update) | async-done | bytes 73744 | tf_op jit(solution)/shard_map/while/body/eval_jaxpr/reduce_scatter | solution.py:66
  52.3 5.6 collective-permute-done.1
  63.0 5.5 all-to-all-done
  73.8 15.0 %reduce-scatter.2.cloned.1.call-done = bf16[32,1152]{1,0:T(8,128)(2,1)} async-done(((bf16[128,1152]{1,0:T(8,128)(2,1)}), bf16[32,1152]{1,0:T(8,128)(2,1)}) %reduce-scatter.2.cloned.1.call-update) | async-done | bytes 73744 | tf_op jit(solution)/shard_map/while/body/eval_jaxpr/reduce_scatter | solution.py:66
  106.0 5.5 all-to-all-done
  116.8 15.0 %reduce-scatter.2.cloned.1.call-done = bf16[32,1152]{1,0:T(8,128)(2,1)} async-done(((bf16[128,1152]{1,0:T(8,128)(2,1)}), bf16[32,1152]{1,0:T(8,128)(2,1)}) %reduce-scatter.2.cloned.1.call-update) | async-done | bytes 73744 | tf_op jit(solution)/shard_map/while/body/eval_jaxpr/reduce_scatter | solution.py:66
  149.0 5.5 all-to-all-done
  159.7 15.0 %reduce-scatter.2.cloned.1.call-done = bf16[32,1152]{1,0:T(8,128)(2,1)} async-done(((bf16[128,1152]{1,0:T(8,128)(2,1)}), bf16[32,1152]{1,0:T(8,128)(2,1)}) %reduce-scatter.2.cloned.1.call-update) | async-done | bytes 73744 | tf_op jit(solution)/shard_map/while/body/eval_jaxpr/reduce_scatter | solution.py:66
  192.1 5.5 all-to-all-done
  202.8 15.0 %reduce-scatter.2.cloned.1.call-done = bf16[32,1152]{1,0:T(8,128)(2,1)} async-done(((bf16[128,1152]{1,0:T(8,128)(2,1)}), bf16[32,1152]{1,0:T(8,128)(2,1)}) %reduce-scatter.2.cloned.1.call-update) | async-done | bytes 73744 | tf_op jit(solution)/shard_map/while/body/eval_jaxpr/reduce_scatter | solution.py:66
  235.0 5.5 all-to-all-done
  245.7 15.0 %reduce-scatter.2.cloned.1.call-done = bf16[32,1152]{1,0:T(8,128)(2,1)} async-done(((bf16[128,1152]{1,0:T(8,128)(2,1)}), bf16[32,1152]{1,0:T(8,128)(2,1)}) %reduce-scatter.2.cloned.1.call-update) | async-done | bytes 73744 | tf_op jit(solution)/shard_map/while/body/eval_jaxpr/reduce_scatter | solution.py:66
  278.0 5.5 all-to-all-done
  288.7 15.0 %reduce-scatter.2.cloned.1.call-done = bf16[32,1152]{1,0:T(8,128)(2,1)} async-done(((bf16[128,1152]{1,0:T(8,128)(2,1)}), bf16[32,1152]{1,0:T(8,128)(2,1)}) %reduce-scatter.2.cloned.1.call-update) | async-done | bytes 73744 | tf_op jit(solution)/shard_map/while/body/eval_jaxpr/reduce_scatter | solution.py:66
  321.0 5.5 all-to-all-done
  331.8 14.9 %reduce-scatter.2.cloned.1.call-done = bf16[32,1152]{1,0:T(8,128)(2,1)} async-done(((bf16[128,1152]{1,0:T(8,128)(2,1)}), bf16[32,1152]{1,0:T(8,128)(2,1)}) %reduce-scatter.2.cloned.1.call-update) | async-done | bytes 73744 | tf_op jit(solution)/shard_map/while/body/eval_jaxpr/reduce_scatter | solution.py:66
  364.0 5.5 all-to-all-done
  374.7 15.0 %reduce-scatter.2.cloned.1.call-done = bf16[32,1152]{1,0:T(8,128)(2,1)} async-done(((bf16[128,1152]{1,0:T(8,128)(2,1)}), bf16[32,1152]{1,0:T(8,128)(2,1)}) %reduce-scatter.2.cloned.1.call-update) | async-done | bytes 73744 | tf_op jit(solution)/shard_map/while/body/eval_jaxpr/reduce_scatter | solution.py:66
  407.0 5.5 all-to-all-done
  417.7 15.0 %reduce-scatter.2.cloned.1.call-done = bf16[32,1152]{1,0:T(8,128)(2,1)} async-done(((bf16[128,1152]{1,0:T(8,128)(2,1)}), bf16[32,1152]{1,0:T(8,128)(2,1)}) %reduce-scatter.2.cloned.1.call-update) | async-done | bytes 73744 | tf_op jit(solution)/shard_map/while/body/eval_jaxpr/reduce_scatter | solution.py:66
  450.0 5.5 all-to-all-done
  460.7 15.0 %reduce-scatter.2.cloned.1.call-done = bf16[32,1152]{1,0:T(8,128)(2,1)} async-done(((bf16[128,1152]{1,0:T(8,128)(2,1)}), bf16[32,1152]{1,0:T(8,128)(2,1)}) %reduce-scatter.2.cloned.1.call-update) | async-done | bytes 73744 | tf_op jit(solution)/shard_map/while/body/eval_jaxpr/reduce_scatter | solution.py:66
  493.0 5.5 all-to-all-done
  503.8 15.0 %reduce-scatter.2.cloned.1.call-done = bf16[32,1152]{1,0:T(8,128)(2,1)} async-done(((bf16[128,1152]{1,0:T(8,128)(2,1)}), bf16[32,1152]{1,0:T(8,128)(2,1)}) %reduce-scatter.2.cloned.1.call-update) | async-done | bytes 73744 | tf_op jit(solution)/shard_map/while/body/eval_jaxpr/reduce_scatter | solution.py:66
  536.0 5.5 all-to-all-done
  546.7 15.0 %reduce-scatter.2.cloned.1.call-done = bf16[32,1152]{1,0:T(8,128)(2,1)} async-done(((bf16[128,1152]{1,0:T(8,128)(2,1)}), bf16[32,1152]{1,0:T(8,128)(2,1)}) %reduce-scatter.2.cloned.1.call-update) | async-done | bytes 73744 | tf_op jit(solution)/shard_map/while/body/eval_jaxpr/reduce_scatter | solution.py:66
  579.0 5.5 all-to-all-done
  589.8 14.9 %reduce-scatter.2.cloned.1.call-done = bf16[32,1152]{1,0:T(8,128)(2,1)} async-done(((bf16[128,1152]{1,0:T(8,128)(2,1)}), bf16[32,1152]{1,0:T(8,128)(2,1)}) %reduce-scatter.2.cloned.1.call-update) | async-done | bytes 73744 | tf_op jit(solution)/shard_map/while/body/eval_jaxpr/reduce_scatter | solution.py:66
  622.0 5.5 all-to-all-done
  632.7 15.0 %reduce-scatter.2.cloned.1.call-done = bf16[32,1152]{1,0:T(8,128)(2,1)} async-done(((bf16[128,1152]{1,0:T(8,128)(2,1)}), bf16[32,1152]{1,0:T(8,128)(2,1)}) %reduce-scatter.2.cloned.1.call-update) | async-done | bytes 73744 | tf_op jit(solution)/shard_map/while/body/eval_jaxpr/reduce_scatter | solution.py:66
  665.0 5.5 all-to-all-done
  675.7 15.0 %reduce-scatter.2.cloned.1.call-done = bf16[32,1152]{1,0:T(8,128)(2,1)} async-done(((bf16[128,1152]{1,0:T(8,128)(2,1)}), bf16[32,1152]{1,0:T(8,128)(2,1)}) %reduce-scatter.2.cloned.1.call-update) | async-done | bytes 73744 | tf_op jit(solution)/shard_map/while/body/eval_jaxpr/reduce_scatter | solution.py:66
  708.0 5.5 all-to-all-done
  718.8 14.9 %reduce-scatter.2.cloned.1.call-done = bf16[32,1152]{1,0:T(8,128)(2,1)} async-done(((bf16[128,1152]{1,0:T(8,128)(2,1)}), bf16[32,1152]{1,0:T(8,128)(2,1)}) %reduce-scatter.2.cloned.1.call-update) | async-done | bytes 73744 | tf_op jit(solution)/shard_map/while/body/eval_jaxpr/reduce_scatter | solution.py:66
  751.0 5.5 all-to-all-done
  761.7 15.0 %reduce-scatter.2.cloned.1.call-done = bf16[32,1152]{1,0:T(8,128)(2,1)} async-done(((bf16[128,1152]{1,0:T(8,128)(2,1)}), bf16[32,1152]{1,0:T(8,128)(2,1)}) %reduce-scatter.2.cloned.1.call-update) | async-done | bytes 73744 | tf_op jit(solution)/shard_map/while/body/eval_jaxpr/reduce_scatter | solution.py:66
  794.0 5.5 all-to-all-done
  804.7 15.0 %reduce-scatter.2.cloned.1.call-done = bf16[32,1152]{1,0:T(8,128)(2,1)} async-done(((bf16[128,1152]{1,0:T(8,128)(2,1)}), bf16[32,1152]{1,0:T(8,128)(2,1)}) %reduce-scatter.2.cloned.1.call-update) | async-done | bytes 73744 | tf_op jit(solution)/shard_map/while/body/eval_jaxpr/reduce_scatter | solution.py:66
  837.0 5.5 all-to-all-done
  847.8 14.9 %reduce-scatter.2.cloned.1.call-done = bf16[32,1152]{1,0:T(8,128)(2,1)} async-done(((bf16[128,1152]{1,0:T(8,128)(2,1)}), bf16[32,1152]{1,0:T(8,128)(2,1)}) %reduce-scatter.2.cloned.1.call-update) | async-done | bytes 73744 | tf_op jit(solution)/shard_map/while/body/eval_jaxpr/reduce_scatter | solution.py:66
  880.0 5.5 all-to-all-done
  890.7 15.0 %reduce-scatter.2.cloned.1.call-done = bf16[32,1152]{1,0:T(8,128)(2,1)} async-done(((bf16[128,1152]{1,0:T(8,128)(2,1)}), bf16[32,1152]{1,0:T(8,128)(2,1)}) %reduce-scatter.2.cloned.1.call-update) | async-done | bytes 73744 | tf_op jit(solution)/shard_map/while/body/eval_jaxpr/reduce_scatter | solution.py:66
  923.0 5.5 all-to-all-done
  933.7 15.0 %reduce-scatter.2.cloned.1.call-done = bf16[32,1152]{1,0:T(8,128)(2,1)} async-done(((bf16[128,1152]{1,0:T(8,128)(2,1)}), bf16[32,1152]{1,0:T(8,128)(2,1)}) %reduce-scatter.2.cloned.1.call-update) | async-done | bytes 73744 | tf_op jit(solution)/shard_map/while/body/eval_jaxpr/reduce_scatter | solution.py:66
  966.0 5.5 all-to-all-done
  976.7 14.9 %reduce-scatter.2.cloned.1.call-done = bf16[32,1152]{1,0:T(8,128)(2,1)} async-done(((bf16[128,1152]{1,0:T(8,128)(2,1)}), bf16[32,1152]{1,0:T(8,128)(2,1)}) %reduce-scatter.2.cloned.1.call-update) | async-done | bytes 73744 | tf_op jit(solution)/shard_map/while/body/eval_jaxpr/reduce_scatter | solution.py:66
  1008.9 5.5 all-to-all-done
  1019.7 15.0 %reduce-scatter.2.cloned.1.call-done = bf16[32,1152]{1,0:T(8,128)(2,1)} async-done(((bf16[128,1152]{1,0:T(8,128)(2,1)}), bf16[32,1152]{1,0:T(8,128)(2,1)}) %reduce-scatter.2.cloned.1.call-update) | async-done | bytes 73744 | tf_op jit(solution)/shard_map/while/body/eval_jaxpr/reduce_scatter | solution.py:66
  1052.0 5.5 all-to-all-done
  1062.7 15.0 %reduce-scatter.2.cloned.1.call-done = bf16[32,1152]{1,0:T(8,128)(2,1)} async-done(((bf16[128,1152]{1,0:T(8,128)(2,1)}), bf16[32,1152]{1,0:T(8,128)(2,1)}) %reduce-scatter.2.cloned.1.call-update) | async-done | bytes 73744 | tf_op jit(solution)/shard_map/while/body/eval_jaxpr/reduce_scatter | solution.py:66
  1095.0 5.5 all-to-all-done
  1105.7 14.9 %reduce-scatter.2.cloned.1.call-done = bf16[32,1152]{1,0:T(8,128)(2,1)} async-done(((bf16[128,1152]{1,0:T(8,128)(2,1)}), bf16[32,1152]{1,0:T(8,128)(2,1)}) %reduce-scatter.2.cloned.1.call-update) | async-done | bytes 73744 | tf_op jit(solution)/shard_map/while/body/eval_jaxpr/reduce_scatter | solution.py:66
  1137.9 5.5 all-to-all-done
  1148.7 15.0 %reduce-scatter.2.cloned.1.call-done = bf16[32,1152]{1,0:T(8,128)(2,1)} async-done(((bf16[128,1152]{1,0:T(8,128)(2,1)}), bf16[32,1152]{1,0:T(8,128)(2,1)}) %reduce-scatter.2.cloned.1.call-update) | async-done | bytes 73744 | tf_op jit(solution)/shard_map/while/body/eval_jaxpr/reduce_scatter | solution.py:66
  1181.0 5.5 all-to-all-done
  1191.7 15.0 %reduce-scatter.2.cloned.1.call-done = bf16[32,1152]{1,0:T(8,128)(2,1)} async-done(((bf16[128,1152]{1,0:T(8,128)(2,1)}), bf16[32,1152]{1,0:T(8,128)(2,1)}) %reduce-scatter.2.cloned.1.call-update) | async-done | bytes 73744 | tf_op jit(solution)/shard_map/while/body/eval_jaxpr/reduce_scatter | solution.py:66
  1224.0 5.5 all-to-all-done
  1234.7 14.9 %reduce-scatter.2.cloned.1.call-done = bf16[32,1152]{1,0:T(8,128)(2,1)} async-done(((bf16[128,1152]{1,0:T(8,128)(2,1)}), bf16[32,1152]{1,0:T(8,128)(2,1)}) %reduce-scatter.2.cloned.1.call-update) | async-done | bytes 73744 | tf_op jit(solution)/shard_map/while/body/eval_jaxpr/reduce_scatter | solution.py:66
  1277.7 15.0 %reduce-scatter.2.cloned.1.call-done = bf16[32,1152]{1,0:T(8,128)(2,1)} async-done(((bf16[128,1152]{1,0:T(8,128)(2,1)}), bf16[32,1152]{1,0:T(8,128)(2,1)}) %reduce-scatter.2.cloned.1.call-update) | async-done | bytes 73744 | tf_op jit(solution)/shard_map/while/body/eval_jaxpr/reduce_scatter | solution.py:66
  1309.9 5.5 all-to-all-done
  1320.7 15.0 %reduce-scatter.2.cloned.1.call-done = bf16[32,1152]{1,0:T(8,128)(2,1)} async-done(((bf16[128,1152]{1,0:T(8,128)(2,1)}), bf16[32,1152]{1,0:T(8,128)(2,1)}) %reduce-scatter.2.cloned.1.call-update) | async-done | bytes 73744 | tf_op jit(solution)/shard_map/while/body/eval_jaxpr/reduce_scatter | solution.py:66
  1363.7 14.9 %reduce-scatter.2.cloned.1.call-done = bf16[32,1152]{1,0:T(8,128)(2,1)} async-done(((bf16[128,1152]{1,0:T(8,128)(2,1)}), bf16[32,1152]{1,0:T(8,128)(2,1)}) %reduce-scatter.2.cloned.1.call-update) | async-done | bytes 73744 | tf_op jit(solution)/shard_map/while/body/eval_jaxpr/reduce_scatter | solution.py:66
  (517 shorter events, 728.9 us)
Async XLA Ops:
  14.5 31.3 %reduce-scatter.2.cloned.1.call-start = ((), (), s32[]{:S(2)}) async-start(), calls=%async_computation.2 | async-start | bytes 368640 | tf_op jit(solution)/shard_map/while/body/eval_jaxpr/reduce_scatter | solution.py:66
  25.1 27.2 %collective-permute-start = (bf16[32,1152]{1,0:T(8,128)(2,1)S(1)}, bf16[32,1152]{1,0:T(8,128)(2,1)S(1)}, u32[]{:S(2)}, u32[]{:S(2)}) collective-permute-start(bf16[32,1152]{1,0:T(8,128)(2,1)S(1)} %copy.13), channel_id=1, source_target_pairs={{0,4},{4,8},{8,12},{12,16},{16,20},{20,24},{24,28},{28,32},{32,36}... | collective-permute-start | bytes 221192 | tf_op jit(solution)/shard_map/while/body/eval_jaxpr/ppermute | solution.py:9
  63.0 25.7 %reduce-scatter.2.cloned.1.call-start = ((), (), s32[]{:S(2)}) async-start(), calls=%async_computation.2 | async-start | bytes 368640 | tf_op jit(solution)/shard_map/while/body/eval_jaxpr/reduce_scatter | solution.py:66
  73.7 24.5 %collective-permute-start = (bf16[32,1152]{1,0:T(8,128)(2,1)S(1)}, bf16[32,1152]{1,0:T(8,128)(2,1)S(1)}, u32[]{:S(2)}, u32[]{:S(2)}) collective-permute-start(bf16[32,1152]{1,0:T(8,128)(2,1)S(1)} %copy.13), channel_id=1, source_target_pairs={{0,4},{4,8},{8,12},{12,16},{16,20},{20,24},{24,28},{28,32},{32,36}... | collective-permute-start | bytes 221192 | tf_op jit(solution)/shard_map/while/body/eval_jaxpr/ppermute | solution.py:9
  106.0 25.7 %reduce-scatter.2.cloned.1.call-start = ((), (), s32[]{:S(2)}) async-start(), calls=%async_computation.2 | async-start | bytes 368640 | tf_op jit(solution)/shard_map/while/body/eval_jaxpr/reduce_scatter | solution.py:66
  116.7 24.5 %collective-permute-start = (bf16[32,1152]{1,0:T(8,128)(2,1)S(1)}, bf16[32,1152]{1,0:T(8,128)(2,1)S(1)}, u32[]{:S(2)}, u32[]{:S(2)}) collective-permute-start(bf16[32,1152]{1,0:T(8,128)(2,1)S(1)} %copy.13), channel_id=1, source_target_pairs={{0,4},{4,8},{8,12},{12,16},{16,20},{20,24},{24,28},{28,32},{32,36}... | collective-permute-start | bytes 221192 | tf_op jit(solution)/shard_map/while/body/eval_jaxpr/ppermute | solution.py:9
  149.0 25.8 %reduce-scatter.2.cloned.1.call-start = ((), (), s32[]{:S(2)}) async-start(), calls=%async_computation.2 | async-start | bytes 368640 | tf_op jit(solution)/shard_map/while/body/eval_jaxpr/reduce_scatter | solution.py:66
  159.7 24.5 %collective-permute-start = (bf16[32,1152]{1,0:T(8,128)(2,1)S(1)}, bf16[32,1152]{1,0:T(8,128)(2,1)S(1)}, u32[]{:S(2)}, u32[]{:S(2)}) collective-permute-start(bf16[32,1152]{1,0:T(8,128)(2,1)S(1)} %copy.13), channel_id=1, source_target_pairs={{0,4},{4,8},{8,12},{12,16},{16,20},{20,24},{24,28},{28,32},{32,36}... | collective-permute-start | bytes 221192 | tf_op jit(solution)/shard_map/while/body/eval_jaxpr/ppermute | solution.py:9
  192.0 25.7 %reduce-scatter.2.cloned.1.call-start = ((), (), s32[]{:S(2)}) async-start(), calls=%async_computation.2 | async-start | bytes 368640 | tf_op jit(solution)/shard_map/while/body/eval_jaxpr/reduce_scatter | solution.py:66
  202.7 24.5 %collective-permute-start = (bf16[32,1152]{1,0:T(8,128)(2,1)S(1)}, bf16[32,1152]{1,0:T(8,128)(2,1)S(1)}, u32[]{:S(2)}, u32[]{:S(2)}) collective-permute-start(bf16[32,1152]{1,0:T(8,128)(2,1)S(1)} %copy.13), channel_id=1, source_target_pairs={{0,4},{4,8},{8,12},{12,16},{16,20},{20,24},{24,28},{28,32},{32,36}... | collective-permute-start | bytes 221192 | tf_op jit(solution)/shard_map/while/body/eval_jaxpr/ppermute | solution.py:9
  235.0 25.7 %reduce-scatter.2.cloned.1.call-start = ((), (), s32[]{:S(2)}) async-start(), calls=%async_computation.2 | async-start | bytes 368640 | tf_op jit(solution)/shard_map/while/body/eval_jaxpr/reduce_scatter | solution.py:66
  245.6 24.5 %collective-permute-start = (bf16[32,1152]{1,0:T(8,128)(2,1)S(1)}, bf16[32,1152]{1,0:T(8,128)(2,1)S(1)}, u32[]{:S(2)}, u32[]{:S(2)}) collective-permute-start(bf16[32,1152]{1,0:T(8,128)(2,1)S(1)} %copy.13), channel_id=1, source_target_pairs={{0,4},{4,8},{8,12},{12,16},{16,20},{20,24},{24,28},{28,32},{32,36}... | collective-permute-start | bytes 221192 | tf_op jit(solution)/shard_map/while/body/eval_jaxpr/ppermute | solution.py:9
  278.0 25.8 %reduce-scatter.2.cloned.1.call-start = ((), (), s32[]{:S(2)}) async-start(), calls=%async_computation.2 | async-start | bytes 368640 | tf_op jit(solution)/shard_map/while/body/eval_jaxpr/reduce_scatter | solution.py:66
  288.6 24.5 %collective-permute-start = (bf16[32,1152]{1,0:T(8,128)(2,1)S(1)}, bf16[32,1152]{1,0:T(8,128)(2,1)S(1)}, u32[]{:S(2)}, u32[]{:S(2)}) collective-permute-start(bf16[32,1152]{1,0:T(8,128)(2,1)S(1)} %copy.13), channel_id=1, source_target_pairs={{0,4},{4,8},{8,12},{12,16},{16,20},{20,24},{24,28},{28,32},{32,36}... | collective-permute-start | bytes 221192 | tf_op jit(solution)/shard_map/while/body/eval_jaxpr/ppermute | solution.py:9
  321.0 25.7 %reduce-scatter.2.cloned.1.call-start = ((), (), s32[]{:S(2)}) async-start(), calls=%async_computation.2 | async-start | bytes 368640 | tf_op jit(solution)/shard_map/while/body/eval_jaxpr/reduce_scatter | solution.py:66
  331.7 24.4 %collective-permute-start = (bf16[32,1152]{1,0:T(8,128)(2,1)S(1)}, bf16[32,1152]{1,0:T(8,128)(2,1)S(1)}, u32[]{:S(2)}, u32[]{:S(2)}) collective-permute-start(bf16[32,1152]{1,0:T(8,128)(2,1)S(1)} %copy.13), channel_id=1, source_target_pairs={{0,4},{4,8},{8,12},{12,16},{16,20},{20,24},{24,28},{28,32},{32,36}... | collective-permute-start | bytes 221192 | tf_op jit(solution)/shard_map/while/body/eval_jaxpr/ppermute | solution.py:9
  364.0 25.8 %reduce-scatter.2.cloned.1.call-start = ((), (), s32[]{:S(2)}) async-start(), calls=%async_computation.2 | async-start | bytes 368640 | tf_op jit(solution)/shard_map/while/body/eval_jaxpr/reduce_scatter | solution.py:66
  374.6 24.5 %collective-permute-start = (bf16[32,1152]{1,0:T(8,128)(2,1)S(1)}, bf16[32,1152]{1,0:T(8,128)(2,1)S(1)}, u32[]{:S(2)}, u32[]{:S(2)}) collective-permute-start(bf16[32,1152]{1,0:T(8,128)(2,1)S(1)} %copy.13), channel_id=1, source_target_pairs={{0,4},{4,8},{8,12},{12,16},{16,20},{20,24},{24,28},{28,32},{32,36}... | collective-permute-start | bytes 221192 | tf_op jit(solution)/shard_map/while/body/eval_jaxpr/ppermute | solution.py:9
  407.0 25.8 %reduce-scatter.2.cloned.1.call-start = ((), (), s32[]{:S(2)}) async-start(), calls=%async_computation.2 | async-start | bytes 368640 | tf_op jit(solution)/shard_map/while/body/eval_jaxpr/reduce_scatter | solution.py:66
  417.6 24.5 %collective-permute-start = (bf16[32,1152]{1,0:T(8,128)(2,1)S(1)}, bf16[32,1152]{1,0:T(8,128)(2,1)S(1)}, u32[]{:S(2)}, u32[]{:S(2)}) collective-permute-start(bf16[32,1152]{1,0:T(8,128)(2,1)S(1)} %copy.13), channel_id=1, source_target_pairs={{0,4},{4,8},{8,12},{12,16},{16,20},{20,24},{24,28},{28,32},{32,36}... | collective-permute-start | bytes 221192 | tf_op jit(solution)/shard_map/while/body/eval_jaxpr/ppermute | solution.py:9
  450.0 25.7 %reduce-scatter.2.cloned.1.call-start = ((), (), s32[]{:S(2)}) async-start(), calls=%async_computation.2 | async-start | bytes 368640 | tf_op jit(solution)/shard_map/while/body/eval_jaxpr/reduce_scatter | solution.py:66
  460.6 24.5 %collective-permute-start = (bf16[32,1152]{1,0:T(8,128)(2,1)S(1)}, bf16[32,1152]{1,0:T(8,128)(2,1)S(1)}, u32[]{:S(2)}, u32[]{:S(2)}) collective-permute-start(bf16[32,1152]{1,0:T(8,128)(2,1)S(1)} %copy.13), channel_id=1, source_target_pairs={{0,4},{4,8},{8,12},{12,16},{16,20},{20,24},{24,28},{28,32},{32,36}... | collective-permute-start | bytes 221192 | tf_op jit(solution)/shard_map/while/body/eval_jaxpr/ppermute | solution.py:9
  493.0 25.7 %reduce-scatter.2.cloned.1.call-start = ((), (), s32[]{:S(2)}) async-start(), calls=%async_computation.2 | async-start | bytes 368640 | tf_op jit(solution)/shard_map/while/body/eval_jaxpr/reduce_scatter | solution.py:66
  503.7 24.4 %collective-permute-start = (bf16[32,1152]{1,0:T(8,128)(2,1)S(1)}, bf16[32,1152]{1,0:T(8,128)(2,1)S(1)}, u32[]{:S(2)}, u32[]{:S(2)}) collective-permute-start(bf16[32,1152]{1,0:T(8,128)(2,1)S(1)} %copy.13), channel_id=1, source_target_pairs={{0,4},{4,8},{8,12},{12,16},{16,20},{20,24},{24,28},{28,32},{32,36}... | collective-permute-start | bytes 221192 | tf_op jit(solution)/shard_map/while/body/eval_jaxpr/ppermute | solution.py:9
  536.0 25.8 %reduce-scatter.2.cloned.1.call-start = ((), (), s32[]{:S(2)}) async-start(), calls=%async_computation.2 | async-start | bytes 368640 | tf_op jit(solution)/shard_map/while/body/eval_jaxpr/reduce_scatter | solution.py:66
  546.6 24.5 %collective-permute-start = (bf16[32,1152]{1,0:T(8,128)(2,1)S(1)}, bf16[32,1152]{1,0:T(8,128)(2,1)S(1)}, u32[]{:S(2)}, u32[]{:S(2)}) collective-permute-start(bf16[32,1152]{1,0:T(8,128)(2,1)S(1)} %copy.13), channel_id=1, source_target_pairs={{0,4},{4,8},{8,12},{12,16},{16,20},{20,24},{24,28},{28,32},{32,36}... | collective-permute-start | bytes 221192 | tf_op jit(solution)/shard_map/while/body/eval_jaxpr/ppermute | solution.py:9
  579.0 25.7 %reduce-scatter.2.cloned.1.call-start = ((), (), s32[]{:S(2)}) async-start(), calls=%async_computation.2 | async-start | bytes 368640 | tf_op jit(solution)/shard_map/while/body/eval_jaxpr/reduce_scatter | solution.py:66
  589.7 24.4 %collective-permute-start = (bf16[32,1152]{1,0:T(8,128)(2,1)S(1)}, bf16[32,1152]{1,0:T(8,128)(2,1)S(1)}, u32[]{:S(2)}, u32[]{:S(2)}) collective-permute-start(bf16[32,1152]{1,0:T(8,128)(2,1)S(1)} %copy.13), channel_id=1, source_target_pairs={{0,4},{4,8},{8,12},{12,16},{16,20},{20,24},{24,28},{28,32},{32,36}... | collective-permute-start | bytes 221192 | tf_op jit(solution)/shard_map/while/body/eval_jaxpr/ppermute | solution.py:9
  622.0 25.8 %reduce-scatter.2.cloned.1.call-start = ((), (), s32[]{:S(2)}) async-start(), calls=%async_computation.2 | async-start | bytes 368640 | tf_op jit(solution)/shard_map/while/body/eval_jaxpr/reduce_scatter | solution.py:66
  632.6 24.5 %collective-permute-start = (bf16[32,1152]{1,0:T(8,128)(2,1)S(1)}, bf16[32,1152]{1,0:T(8,128)(2,1)S(1)}, u32[]{:S(2)}, u32[]{:S(2)}) collective-permute-start(bf16[32,1152]{1,0:T(8,128)(2,1)S(1)} %copy.13), channel_id=1, source_target_pairs={{0,4},{4,8},{8,12},{12,16},{16,20},{20,24},{24,28},{28,32},{32,36}... | collective-permute-start | bytes 221192 | tf_op jit(solution)/shard_map/while/body/eval_jaxpr/ppermute | solution.py:9
  665.0 25.8 %reduce-scatter.2.cloned.1.call-start = ((), (), s32[]{:S(2)}) async-start(), calls=%async_computation.2 | async-start | bytes 368640 | tf_op jit(solution)/shard_map/while/body/eval_jaxpr/reduce_scatter | solution.py:66
  675.6 24.5 %collective-permute-start = (bf16[32,1152]{1,0:T(8,128)(2,1)S(1)}, bf16[32,1152]{1,0:T(8,128)(2,1)S(1)}, u32[]{:S(2)}, u32[]{:S(2)}) collective-permute-start(bf16[32,1152]{1,0:T(8,128)(2,1)S(1)} %copy.13), channel_id=1, source_target_pairs={{0,4},{4,8},{8,12},{12,16},{16,20},{20,24},{24,28},{28,32},{32,36}... | collective-permute-start | bytes 221192 | tf_op jit(solution)/shard_map/while/body/eval_jaxpr/ppermute | solution.py:9
  708.0 25.7 %reduce-scatter.2.cloned.1.call-start = ((), (), s32[]{:S(2)}) async-start(), calls=%async_computation.2 | async-start | bytes 368640 | tf_op jit(solution)/shard_map/while/body/eval_jaxpr/reduce_scatter | solution.py:66
  718.7 24.4 %collective-permute-start = (bf16[32,1152]{1,0:T(8,128)(2,1)S(1)}, bf16[32,1152]{1,0:T(8,128)(2,1)S(1)}, u32[]{:S(2)}, u32[]{:S(2)}) collective-permute-start(bf16[32,1152]{1,0:T(8,128)(2,1)S(1)} %copy.13), channel_id=1, source_target_pairs={{0,4},{4,8},{8,12},{12,16},{16,20},{20,24},{24,28},{28,32},{32,36}... | collective-permute-start | bytes 221192 | tf_op jit(solution)/shard_map/while/body/eval_jaxpr/ppermute | solution.py:9
  751.0 25.8 %reduce-scatter.2.cloned.1.call-start = ((), (), s32[]{:S(2)}) async-start(), calls=%async_computation.2 | async-start | bytes 368640 | tf_op jit(solution)/shard_map/while/body/eval_jaxpr/reduce_scatter | solution.py:66
  761.6 24.5 %collective-permute-start = (bf16[32,1152]{1,0:T(8,128)(2,1)S(1)}, bf16[32,1152]{1,0:T(8,128)(2,1)S(1)}, u32[]{:S(2)}, u32[]{:S(2)}) collective-permute-start(bf16[32,1152]{1,0:T(8,128)(2,1)S(1)} %copy.13), channel_id=1, source_target_pairs={{0,4},{4,8},{8,12},{12,16},{16,20},{20,24},{24,28},{28,32},{32,36}... | collective-permute-start | bytes 221192 | tf_op jit(solution)/shard_map/while/body/eval_jaxpr/ppermute | solution.py:9
  794.0 25.8 %reduce-scatter.2.cloned.1.call-start = ((), (), s32[]{:S(2)}) async-start(), calls=%async_computation.2 | async-start | bytes 368640 | tf_op jit(solution)/shard_map/while/body/eval_jaxpr/reduce_scatter | solution.py:66
  804.6 24.5 %collective-permute-start = (bf16[32,1152]{1,0:T(8,128)(2,1)S(1)}, bf16[32,1152]{1,0:T(8,128)(2,1)S(1)}, u32[]{:S(2)}, u32[]{:S(2)}) collective-permute-start(bf16[32,1152]{1,0:T(8,128)(2,1)S(1)} %copy.13), channel_id=1, source_target_pairs={{0,4},{4,8},{8,12},{12,16},{16,20},{20,24},{24,28},{28,32},{32,36}... | collective-permute-start | bytes 221192 | tf_op jit(solution)/shard_map/while/body/eval_jaxpr/ppermute | solution.py:9
  837.0 25.7 %reduce-scatter.2.cloned.1.call-start = ((), (), s32[]{:S(2)}) async-start(), calls=%async_computation.2 | async-start | bytes 368640 | tf_op jit(solution)/shard_map/while/body/eval_jaxpr/reduce_scatter | solution.py:66
  847.7 24.4 %collective-permute-start = (bf16[32,1152]{1,0:T(8,128)(2,1)S(1)}, bf16[32,1152]{1,0:T(8,128)(2,1)S(1)}, u32[]{:S(2)}, u32[]{:S(2)}) collective-permute-start(bf16[32,1152]{1,0:T(8,128)(2,1)S(1)} %copy.13), channel_id=1, source_target_pairs={{0,4},{4,8},{8,12},{12,16},{16,20},{20,24},{24,28},{28,32},{32,36}... | collective-permute-start | bytes 221192 | tf_op jit(solution)/shard_map/while/body/eval_jaxpr/ppermute | solution.py:9
  879.9 25.8 %reduce-scatter.2.cloned.1.call-start = ((), (), s32[]{:S(2)}) async-start(), calls=%async_computation.2 | async-start | bytes 368640 | tf_op jit(solution)/shard_map/while/body/eval_jaxpr/reduce_scatter | solution.py:66
  890.6 24.5 %collective-permute-start = (bf16[32,1152]{1,0:T(8,128)(2,1)S(1)}, bf16[32,1152]{1,0:T(8,128)(2,1)S(1)}, u32[]{:S(2)}, u32[]{:S(2)}) collective-permute-start(bf16[32,1152]{1,0:T(8,128)(2,1)S(1)} %copy.13), channel_id=1, source_target_pairs={{0,4},{4,8},{8,12},{12,16},{16,20},{20,24},{24,28},{28,32},{32,36}... | collective-permute-start | bytes 221192 | tf_op jit(solution)/shard_map/while/body/eval_jaxpr/ppermute | solution.py:9
  923.0 25.8 %reduce-scatter.2.cloned.1.call-start = ((), (), s32[]{:S(2)}) async-start(), calls=%async_computation.2 | async-start | bytes 368640 | tf_op jit(solution)/shard_map/while/body/eval_jaxpr/reduce_scatter | solution.py:66
  933.6 24.5 %collective-permute-start = (bf16[32,1152]{1,0:T(8,128)(2,1)S(1)}, bf16[32,1152]{1,0:T(8,128)(2,1)S(1)}, u32[]{:S(2)}, u32[]{:S(2)}) collective-permute-start(bf16[32,1152]{1,0:T(8,128)(2,1)S(1)} %copy.13), channel_id=1, source_target_pairs={{0,4},{4,8},{8,12},{12,16},{16,20},{20,24},{24,28},{28,32},{32,36}... | collective-permute-start | bytes 221192 | tf_op jit(solution)/shard_map/while/body/eval_jaxpr/ppermute | solution.py:9
  966.0 25.7 %reduce-scatter.2.cloned.1.call-start = ((), (), s32[]{:S(2)}) async-start(), calls=%async_computation.2 | async-start | bytes 368640 | tf_op jit(solution)/shard_map/while/body/eval_jaxpr/reduce_scatter | solution.py:66
  976.7 24.4 %collective-permute-start = (bf16[32,1152]{1,0:T(8,128)(2,1)S(1)}, bf16[32,1152]{1,0:T(8,128)(2,1)S(1)}, u32[]{:S(2)}, u32[]{:S(2)}) collective-permute-start(bf16[32,1152]{1,0:T(8,128)(2,1)S(1)} %copy.13), channel_id=1, source_target_pairs={{0,4},{4,8},{8,12},{12,16},{16,20},{20,24},{24,28},{28,32},{32,36}... | collective-permute-start | bytes 221192 | tf_op jit(solution)/shard_map/while/body/eval_jaxpr/ppermute | solution.py:9
  1008.9 25.8 %reduce-scatter.2.cloned.1.call-start = ((), (), s32[]{:S(2)}) async-start(), calls=%async_computation.2 | async-start | bytes 368640 | tf_op jit(solution)/shard_map/while/body/eval_jaxpr/reduce_scatter | solution.py:66
  1019.6 24.5 %collective-permute-start = (bf16[32,1152]{1,0:T(8,128)(2,1)S(1)}, bf16[32,1152]{1,0:T(8,128)(2,1)S(1)}, u32[]{:S(2)}, u32[]{:S(2)}) collective-permute-start(bf16[32,1152]{1,0:T(8,128)(2,1)S(1)} %copy.13), channel_id=1, source_target_pairs={{0,4},{4,8},{8,12},{12,16},{16,20},{20,24},{24,28},{28,32},{32,36}... | collective-permute-start | bytes 221192 | tf_op jit(solution)/shard_map/while/body/eval_jaxpr/ppermute | solution.py:9
  1052.0 25.8 %reduce-scatter.2.cloned.1.call-start = ((), (), s32[]{:S(2)}) async-start(), calls=%async_computation.2 | async-start | bytes 368640 | tf_op jit(solution)/shard_map/while/body/eval_jaxpr/reduce_scatter | solution.py:66
  1062.6 24.5 %collective-permute-start = (bf16[32,1152]{1,0:T(8,128)(2,1)S(1)}, bf16[32,1152]{1,0:T(8,128)(2,1)S(1)}, u32[]{:S(2)}, u32[]{:S(2)}) collective-permute-start(bf16[32,1152]{1,0:T(8,128)(2,1)S(1)} %copy.13), channel_id=1, source_target_pairs={{0,4},{4,8},{8,12},{12,16},{16,20},{20,24},{24,28},{28,32},{32,36}... | collective-permute-start | bytes 221192 | tf_op jit(solution)/shard_map/while/body/eval_jaxpr/ppermute | solution.py:9
  1095.0 25.7 %reduce-scatter.2.cloned.1.call-start = ((), (), s32[]{:S(2)}) async-start(), calls=%async_computation.2 | async-start | bytes 368640 | tf_op jit(solution)/shard_map/while/body/eval_jaxpr/reduce_scatter | solution.py:66
  1105.7 24.4 %collective-permute-start = (bf16[32,1152]{1,0:T(8,128)(2,1)S(1)}, bf16[32,1152]{1,0:T(8,128)(2,1)S(1)}, u32[]{:S(2)}, u32[]{:S(2)}) collective-permute-start(bf16[32,1152]{1,0:T(8,128)(2,1)S(1)} %copy.13), channel_id=1, source_target_pairs={{0,4},{4,8},{8,12},{12,16},{16,20},{20,24},{24,28},{28,32},{32,36}... | collective-permute-start | bytes 221192 | tf_op jit(solution)/shard_map/while/body/eval_jaxpr/ppermute | solution.py:9
  1137.9 25.8 %reduce-scatter.2.cloned.1.call-start = ((), (), s32[]{:S(2)}) async-start(), calls=%async_computation.2 | async-start | bytes 368640 | tf_op jit(solution)/shard_map/while/body/eval_jaxpr/reduce_scatter | solution.py:66
  1148.6 24.5 %collective-permute-start = (bf16[32,1152]{1,0:T(8,128)(2,1)S(1)}, bf16[32,1152]{1,0:T(8,128)(2,1)S(1)}, u32[]{:S(2)}, u32[]{:S(2)}) collective-permute-start(bf16[32,1152]{1,0:T(8,128)(2,1)S(1)} %copy.13), channel_id=1, source_target_pairs={{0,4},{4,8},{8,12},{12,16},{16,20},{20,24},{24,28},{28,32},{32,36}... | collective-permute-start | bytes 221192 | tf_op jit(solution)/shard_map/while/body/eval_jaxpr/ppermute | solution.py:9
  1180.9 25.8 %reduce-scatter.2.cloned.1.call-start = ((), (), s32[]{:S(2)}) async-start(), calls=%async_computation.2 | async-start | bytes 368640 | tf_op jit(solution)/shard_map/while/body/eval_jaxpr/reduce_scatter | solution.py:66
  1191.6 24.5 %collective-permute-start = (bf16[32,1152]{1,0:T(8,128)(2,1)S(1)}, bf16[32,1152]{1,0:T(8,128)(2,1)S(1)}, u32[]{:S(2)}, u32[]{:S(2)}) collective-permute-start(bf16[32,1152]{1,0:T(8,128)(2,1)S(1)} %copy.13), channel_id=1, source_target_pairs={{0,4},{4,8},{8,12},{12,16},{16,20},{20,24},{24,28},{28,32},{32,36}... | collective-permute-start | bytes 221192 | tf_op jit(solution)/shard_map/while/body/eval_jaxpr/ppermute | solution.py:9
  1224.0 25.7 %reduce-scatter.2.cloned.1.call-start = ((), (), s32[]{:S(2)}) async-start(), calls=%async_computation.2 | async-start | bytes 368640 | tf_op jit(solution)/shard_map/while/body/eval_jaxpr/reduce_scatter | solution.py:66
  1234.6 24.4 %collective-permute-start = (bf16[32,1152]{1,0:T(8,128)(2,1)S(1)}, bf16[32,1152]{1,0:T(8,128)(2,1)S(1)}, u32[]{:S(2)}, u32[]{:S(2)}) collective-permute-start(bf16[32,1152]{1,0:T(8,128)(2,1)S(1)} %copy.13), channel_id=1, source_target_pairs={{0,4},{4,8},{8,12},{12,16},{16,20},{20,24},{24,28},{28,32},{32,36}... | collective-permute-start | bytes 221192 | tf_op jit(solution)/shard_map/while/body/eval_jaxpr/ppermute | solution.py:9
  1266.9 25.8 %reduce-scatter.2.cloned.1.call-start = ((), (), s32[]{:S(2)}) async-start(), calls=%async_computation.2 | async-start | bytes 368640 | tf_op jit(solution)/shard_map/while/body/eval_jaxpr/reduce_scatter | solution.py:66
  1277.6 24.5 %collective-permute-start = (bf16[32,1152]{1,0:T(8,128)(2,1)S(1)}, bf16[32,1152]{1,0:T(8,128)(2,1)S(1)}, u32[]{:S(2)}, u32[]{:S(2)}) collective-permute-start(bf16[32,1152]{1,0:T(8,128)(2,1)S(1)} %copy.13), channel_id=1, source_target_pairs={{0,4},{4,8},{8,12},{12,16},{16,20},{20,24},{24,28},{28,32},{32,36}... | collective-permute-start | bytes 221192 | tf_op jit(solution)/shard_map/while/body/eval_jaxpr/ppermute | solution.py:9
  1309.9 25.8 %reduce-scatter.2.cloned.1.call-start = ((), (), s32[]{:S(2)}) async-start(), calls=%async_computation.2 | async-start | bytes 368640 | tf_op jit(solution)/shard_map/while/body/eval_jaxpr/reduce_scatter | solution.py:66
  1320.6 24.5 %collective-permute-start = (bf16[32,1152]{1,0:T(8,128)(2,1)S(1)}, bf16[32,1152]{1,0:T(8,128)(2,1)S(1)}, u32[]{:S(2)}, u32[]{:S(2)}) collective-permute-start(bf16[32,1152]{1,0:T(8,128)(2,1)S(1)} %copy.13), channel_id=1, source_target_pairs={{0,4},{4,8},{8,12},{12,16},{16,20},{20,24},{24,28},{28,32},{32,36}... | collective-permute-start | bytes 221192 | tf_op jit(solution)/shard_map/while/body/eval_jaxpr/ppermute | solution.py:9
  1353.0 25.7 %reduce-scatter.2.cloned.1.call-start = ((), (), s32[]{:S(2)}) async-start(), calls=%async_computation.2 | async-start | bytes 368640 | tf_op jit(solution)/shard_map/while/body/eval_jaxpr/reduce_scatter | solution.py:66
  1363.6 24.4 %collective-permute-start = (bf16[32,1152]{1,0:T(8,128)(2,1)S(1)}, bf16[32,1152]{1,0:T(8,128)(2,1)S(1)}, u32[]{:S(2)}, u32[]{:S(2)}) collective-permute-start(bf16[32,1152]{1,0:T(8,128)(2,1)S(1)} %copy.13), channel_id=1, source_target_pairs={{0,4},{4,8},{8,12},{12,16},{16,20},{20,24},{24,28},{28,32},{32,36}... | collective-permute-start | bytes 221192 | tf_op jit(solution)/shard_map/while/body/eval_jaxpr/ppermute | solution.py:9
  (96 other events, 1143.9 us)
Sparse Core Ops, SparseCore 0:
  25.2 20.4 reduce-scatter.1
  73.8 14.9 reduce-scatter.1
  116.8 14.9 reduce-scatter.1
  159.8 14.9 reduce-scatter.1
  202.8 14.8 reduce-scatter.1
  245.8 14.9 reduce-scatter.1
  288.8 14.9 reduce-scatter.1
  331.8 14.8 reduce-scatter.1
  374.7 14.9 reduce-scatter.1
  417.8 14.9 reduce-scatter.1
  460.8 14.9 reduce-scatter.1
  503.8 14.8 reduce-scatter.1
  546.8 14.9 reduce-scatter.1
  589.8 14.8 reduce-scatter.1
  632.7 14.9 reduce-scatter.1
  675.7 14.9 reduce-scatter.1
  718.8 14.8 reduce-scatter.1
  761.7 14.9 reduce-scatter.1
  804.7 14.9 reduce-scatter.1
  847.8 14.8 reduce-scatter.1
  890.7 14.9 reduce-scatter.1
  933.7 14.9 reduce-scatter.1
  976.8 14.8 reduce-scatter.1
  1019.7 14.9 reduce-scatter.1
  1062.7 14.9 reduce-scatter.1
  1105.8 14.8 reduce-scatter.1
  1148.7 14.9 reduce-scatter.1
  1191.7 14.9 reduce-scatter.1
  1234.8 14.8 reduce-scatter.1
  1277.7 14.9 reduce-scatter.1
  1320.7 14.9 reduce-scatter.1
  1363.8 14.8 reduce-scatter.1
